TPU v7x, 32 devices: a whole 2x2x4 slice. The times are simulated.
32 devices in a mesh: blk: 4 (over y, core), batch: 8 (over z, x).
Axes of the slice: x: 2, y: 2, z: 4, core: 2. Of those that a mesh axis runs over, the one named last changes fastest.
Arguments:
- tokens: bfloat16 [32, 512, 768], P('batch', 'blk'), may hold values from -6 to 6
- cotangent: bfloat16 [32, 512, 768], P('batch', 'blk'), may hold values from -6 to 6
- span_mask: int32 [32, 512], P('batch', 'blk'), may hold values from 0 to 1, as said below
- attention_weight: float32 [4, 768, 768], P(None, 'blk', 'batch'), may hold values from -2 to 2
- expand_weight: float32 [768, 3072], P('blk', 'batch'), may hold values from -0.21875 to 0.21875
- reduce_weight: float32 [3072, 768], P('blk', 'batch'), may hold values from -0.109375 to 0.109375
- vectors: float32 [12, 768], P('blk', 'batch'), may hold values from -2 to 2
- attention_first: float32 [4, 768, 768], P(None, 'blk', 'batch'), may hold values from -40 to 40
- attention_second: float32 [4, 768, 768], P(None, 'blk', 'batch'), may hold values from 0 to 11
- expand_first: float32 [768, 3072], P('blk', 'batch'), may hold values from -40 to 40
- expand_second: float32 [768, 3072], P('blk', 'batch'), may hold values from 0 to 11
- reduce_first: float32 [3072, 768], P('blk', 'batch'), may hold values from -40 to 40
- reduce_second: float32 [3072, 768], P('blk', 'batch'), may hold values from 0 to 11
- vector_first: float32 [12, 768], P('blk', 'batch'), may hold values from -40 to 40
- vector_second: float32 [12, 768], P('blk', 'batch'), may hold values from 0 to 11
Outputs:
- out_tokens: bfloat16 [32, 512, 768], P('batch', 'blk')
- input_grad: float32 [32, 512, 768], P('batch', 'blk')
- attention_new: float32 [4, 768, 768], P(None, 'blk', 'batch')
- attention_moment_one: float32 [4, 768, 768], P(None, 'blk', 'batch')
- attention_moment_two: float32 [4, 768, 768], P(None, 'blk', 'batch')
- expand_new: float32 [768, 3072], P('blk', 'batch')
- expand_moment_one: float32 [768, 3072], P('blk', 'batch')
- expand_moment_two: float32 [768, 3072], P('blk', 'batch')
- reduce_new: float32 [3072, 768], P('blk', 'batch')
- reduce_moment_one: float32 [3072, 768], P('blk', 'batch')
- reduce_moment_two: float32 [3072, 768], P('blk', 'batch')
- vector_new: float32 [12, 768], P('blk', 'batch')
- vector_moment_one: float32 [12, 768], P('blk', 'batch')
- vector_moment_two: float32 [12, 768], P('blk', 'batch')
Inputs may be any that keep to these rules, and one draw needn't show every extreme that they name: `span_mask`: 1 marks a character inside a masked span; spans are aligned runs of 8 characters, each masked with a probability of 5 to 25 percent drawn for its row.
All inputs are finite; a program needn't handle non-finite values.
Results may differ from a plain program's by a relative error of at most 0.019.
Values may be sent and summed in bfloat16 or wider, within the bound.
A program may use at most 192 MiB of HBM per device.

v0:
```python
import functools
import math

import jax
import jax.numpy as jnp
from jax import lax
from jax.experimental import pallas as pl
from jax.experimental.pallas import tpu as pltpu
from jax.sharding import PartitionSpec as P

HEADS = 12
HEAD = 64
STEP = 10
GROUPS = 8

norm_epsilon = 1e-05
beta_one = 0.9
beta_two = 0.999
adam_epsilon = 1e-08
decay_weight = 0.1
rate_attention = 0.05
rate_expand = 0.03
rate_reduce = 0.015
rate_vector = 0.4

F32 = jnp.float32
BF16 = jnp.bfloat16
MESH = pl.DeviceIdType.MESH
GELU_SCALE = math.sqrt(2.0 / math.pi)
GELU_CUBE = 0.044715


def adamw(weight, moment_one, moment_two, gradient, step_rate):
    moment_one = beta_one * moment_one + (1.0 - beta_one) * gradient
    moment_two = beta_two * moment_two + (1.0 - beta_two) * gradient * gradient
    corrected_one = moment_one / (1.0 - beta_one**STEP)
    corrected_two = moment_two / (1.0 - beta_two**STEP)
    updated = weight - step_rate * (
        corrected_one / (jnp.sqrt(corrected_two) + adam_epsilon) + decay_weight * weight
    )
    return (updated, moment_one, moment_two)


def dot_nn(left, right):
    return lax.dot_general(left, right, (((1,), (0,)), ((), ())), preferred_element_type=F32)


def dot_nt(left, right):
    return lax.dot_general(left, right, (((1,), (1,)), ((), ())), preferred_element_type=F32)


X, Y, Z = 1, 2, 4
(N_QKA, N_QKB, N_VOA, N_VOB, N_W10A, N_W10B, N_W11A, N_W11B, N_W20A, N_W20B, N_W21A, N_W21B) = range(12)
(N_AQKA, N_AQKB, N_AVOA, N_AVOB, N_G10, N_G11, N_G20, N_G21) = range(8)
QK, VO = (N_QKA, N_QKB), (N_VOA, N_VOB)
AQK, AVO = (N_AQKA, N_AQKB), (N_AVOA, N_AVOB)
SEND, GOT, WHOLE, SUM, VEC, SMALL, DO = range(7)
(TOK, COT, OUT, IG, TOK_HERE, COT_HERE, OUT_HERE,
 IG_HERE, SWAP_HERE, N2S_HERE, COTS_HERE, BACKS_HERE, AHEADS_HERE) = range(13)
GATHER_ROUTES = (
    ((Z, X, Y), (Z, Y, X),),
    ((Z, Y, X), (Z, Y, X),),
    ((Y, Z, X), (Y, Z, X),),
    ((X, Z, Y), (Z, Y, X),),
    ((Z, Y, X), (Z, Y, X),),
    ((Z, X, Y), (X, Y, Z),),
)
SUM_ROUTES = (
    ((Y, X, Z), (X, Z, Y),),
    ((Y, X, Z), (X, Z, Y),),
    ((Y, X, Z),),
    ((X, Y, Z),),
    ((Z, Y, X),),
    ((Y, Z, X),),
)
PLAN = dict(
    own1=(
        (SEND, N_QKA, 0, X), (SEND, N_QKA, 0, Z), (SEND, N_QKB, 0, X), (SEND, N_QKB, 0, Y),
        (SEND, N_QKB, 0, Z),
    ),
    ownff=(
        (SEND, N_VOA, 0, X), (SEND, N_VOB, 0, X), (DO, TOK), (SEND, N_VOA, 0, Z), (VEC, 0), (DO, SWAP_HERE),
        (GOT, N_QKA, X),
    ),
    mask=(
        (GOT, N_QKB, Y), (SEND, N_QKB, Y, X), (GOT, N_QKB, X), (SEND, N_W10A, 0, X), (SEND, N_W11A, 0, X),
    ),
    ln1=(
        (GOT, N_VOA, X), (VEC, 1), (GOT, N_QKA, Z), (GOT, N_VOB, X), (SEND, N_QKA, Z, X), (SEND, N_VOB, 0, Z),
        (GOT, N_QKB, Y | X), (SEND, N_W10B, 0, X), (GOT, N_W11A, X), (VEC, 2), (SEND, N_QKA, Z, Y),
        (GOT, N_QKB, Z), (SEND, N_QKB, Z, X), (SEND, N_QKB, Z, Y), (SEND, N_W11B, 0, Z), (GOT, N_QKA, Z | X),
        (SEND, N_W11B, 0, X), (SEND, N_QKA, Z | X, Y), (GOT, N_W10A, X), (GOT, N_VOA, Z), (SEND, N_VOA, Z, X),
        (DO, TOK_HERE), (SEND, N_W10A, 0, Z), (SEND, N_QKA, 0, Y), (GOT, N_QKB, Z | X), (SEND, N_QKA, X, Y),
        (GOT, N_W10B, X), (GOT, N_QKB, Z | Y), (SEND, N_QKB, Z | Y, X), (SEND, N_VOA, Z, Y), (GOT, N_VOB, Z),
        (SEND, N_VOB, Z, X), (VEC, 3), (SEND, N_W10B, 0, Z),
    ),
    unp0=(
        (GOT, N_VOA, Z | X), (GOT, N_QKA, Z | Y), (SEND, N_VOB, Z, Y), (GOT, N_W11B, X), (SEND, N_W21B, 0, X),
        (GOT, N_W11B, Z), (SEND, N_W11B, Z, X), (GOT, N_QKA, Z | X | Y), (SEND, N_W11A, 0, Z),
        (SEND, N_VOA, 0, Y), (GOT, N_QKB, Z | Y | X), (GOT, N_QKA, Y), (SEND, N_VOB, 0, Y),
        (GOT, N_QKA, X | Y), (SEND, N_W10A, 0, Y), (SEND, N_W10B, 0, Y), (GOT, N_VOB, Z | X),
        (GOT, N_W10A, Z), (SEND, N_W10A, Z, X), (SEND, N_W11A, X, Z), (SEND, N_W11B, Z, Y), (WHOLE, N_QKA),
        (WHOLE, N_QKB), (GOT, N_VOA, Z | Y), (SEND, N_VOA, Z | Y, X),
    ),
    projk=(
        (GOT, N_W11B, Z | X), (SEND, N_W11B, 0, Y),
    ),
    attend0=(
        (GOT, N_W21B, X), (GOT, N_W10B, Z), (GOT, N_VOB, Z | Y), (SEND, N_VOB, Z | Y, X), (DO, COT),
    ),
    attend1=(
        (GOT, N_VOA, Y), (SEND, N_VOA, Y, X), (GOT, N_VOB, Y), (SEND, N_VOB, Y, X),
    ),
    attend2=(
        (GOT, N_W10A, Z | X), (SEND, N_W10B, Z, X), (GOT, N_W10A, Y), (SEND, N_W10A, Y, Z),
    ),
    attend3=(
        (GOT, N_W11A, Z), (GOT, N_W10B, Y), (SEND, N_W10B, Y, Z),
    ),
    attend4=(
        (GOT, N_VOA, Z | Y | X),
    ),
    attend5=(
        (GOT, N_W11B, Z | Y), (SEND, N_W11B, Z | Y, X), (GOT, N_W11A, X | Z), (GOT, N_W11B, Y),
        (SEND, N_W20A, 0, Z),
    ),
    unp1=(
        (GOT, N_VOB, Z | Y | X), (GOT, N_VOA, Y | X), (GOT, N_VOB, Y | X), (SEND, N_W11A, Z, Y),
        (GOT, N_W10A, Y | Z), (SEND, N_W10A, Y | Z, X), (SEND, N_W20B, 0, Z), (WHOLE, N_VOA), (WHOLE, N_VOB),
        (GOT, N_W10B, Z | X),
    ),
    projv=(
        (SEND, N_W11A, X | Z, Y),
    ),
    mix0=(
        (SEND, N_W10A, Y, X), (SEND, N_W10B, Y, X),
    ),
    mix1=(
        (GOT, N_W10B, Y | Z), (SEND, N_W10B, Y | Z, X), (SEND, N_W21A, 0, Z),
    ),
    mix3=(
        (GOT, N_W11B, Z | Y | X), (SEND, N_W11B, Y, X), (SEND, N_W11A, 0, Y),
    ),
    ao=(
        (SEND, N_W21A, 0, X), (SEND, N_W11A, X, Y),
    ),
    ln2=(
        (DO, COT_HERE),
    ),
    expa0=(
        (GOT, N_W10A, Y | Z | X), (GOT, N_W20A, Z), (SEND, N_W20A, Z, X), (SEND, N_W20A, Z, Y),
        (SEND, N_W21B, 0, Z), (GOT, N_W11A, Z | Y), (GOT, N_W10B, Y | Z | X), (DO, COTS_HERE),
        (GOT, N_W10A, Y | X), (GOT, N_W20B, Z), (SEND, N_W20B, Z, X), (SEND, N_W20B, Z, Y),
        (SEND, N_W21B, X, Z), (GOT, N_W10B, Y | X), (GOT, N_W11A, X | Z | Y), (DO, N2S_HERE),
        (SEND, N_W21B, 0, Y), (GOT, N_W11B, Y | X), (GOT, N_W11A, Y), (SEND, N_W21B, X, Y), (GOT, N_W21A, X),
        (GOT, N_W11A, X | Y), (SEND, N_W20A, 0, Y),
    ),
    expa1=(
        (GOT, N_W21A, Z), (SEND, N_W21A, Z, X), (SEND, N_W20B, 0, Y), (SEND, N_W21A, Z, Y),
        (GOT, N_W20A, Z | X), (GOT, N_W20A, Z | Y), (SEND, N_W20A, Z | Y, X),
    ),
    expb0=(
        (GOT, N_W21B, Z),
    ),
    expb1=(
        (GOT, N_W20B, Z | X), (GOT, N_W20B, Z | Y), (SEND, N_W20B, Z | Y, X), (GOT, N_W21B, Y),
        (SEND, N_W21B, Y, Z), (SEND, N_W20A, 0, X), (GOT, N_W21B, X | Y), (SEND, N_W21B, X | Y, Z),
        (SEND, N_W20B, 0, X), (SEND, N_W21A, 0, Y),
    ),
    trY=(
        (GOT, N_W21A, Z | X), (SEND, N_W21A, Z | X, Y), (GOT, N_W20A, Y), (SEND, N_W20A, Y, X),
        (GOT, N_W21B, X | Z), (SEND, N_W21A, X, Y), (GOT, N_W20B, Y), (SEND, N_W20B, Y, X),
    ),
    gw2_0=(
        (GOT, N_W20A, Z | Y | X),
    ),
    gw2_1=(
        (GOT, N_W21A, Z | Y), (GOT, N_W21B, Y | Z), (GOT, N_W20B, Z | Y | X),
    ),
    innb0=(
        (GOT, N_W20A, X), (GOT, N_W21A, Z | X | Y), (GOT, N_W20B, X), (GOT, N_W21A, Y), (SUM, N_G20, 0),
        (SUM, N_G21, 0), (GOT, N_W21B, X | Y | Z), (GOT, N_W20A, Y | X), (GOT, N_W21A, X | Y),
        (GOT, N_W20B, Y | X),
    ),
    gw1_0=(
        (DO, BACKS_HERE),
    ),
    hid=(
        (SUM, N_G10, 0), (SUM, N_G11, 0),
    ),
    dO=(
        (SUM, N_G21, 1),
    ),
    ab4=(
        (SUM, N_G20, 1),
    ),
    ab5=(
        (SUM, N_G10, 1), (SUM, N_G11, 1),
    ),
    gaqk=(
        (SUM, N_G20, 2),
    ),
    reda=(
        (SUM, N_AVOB, 0), (SUM, N_G10, 2), (SUM, N_AVOA, 0),
    ),
    outst=(
        (SUM, N_G20, 3), (SUM, N_G11, 2), (SUM, N_AQKB, 0), (SUM, N_G21, 2), (SUM, N_AQKA, 0),
        (DO, AHEADS_HERE),
    ),
    end=(
        (SUM, N_AVOB, 1), (SUM, N_AVOA, 1), (SUM, N_G10, 3), (DO, OUT), (SUM, N_AQKB, 1), (SUM, N_AQKA, 1),
        (SUM, N_G11, 3), (SMALL, 0), (SUM, N_AVOA, 2), (SMALL, 1), (DO, IG), (SUM, N_G21, 3),
        (SUM, N_AVOB, 2), (SUM, N_AQKA, 2), (SMALL, 2), (DO, OUT_HERE), (SUM, N_AQKB, 2), (SUM, N_AVOA, 3),
        (DO, IG_HERE), (SUM, N_AVOB, 3), (SUM, N_AQKB, 3), (SUM, N_AQKA, 3), (SMALL, 3),
    ),
)


def lane_tiles(ref, count=6):
    return jnp.concatenate([ref[t] for t in range(count)], axis=1)


class Unit:
    def __init__(self, index, route, rows, u, other):
        self.index, self.route, self.rows, self.u, self.other = index, route, rows, u, other


class Gradient:
    def __init__(self, index, route, rows, u, other, core_in, got, total):
        self.index, self.route, self.rows, self.u, self.other = index, route, rows, u, other
        self.core_in, self.got, self.total = core_in, got, total


def kernel(sub, zs, *refs):
    (tok, cot, mask_in, vec_in, a_in, w1_in, w2_in,
     out, ig, ga, g1, g2, gv,
     ua, uw1, uw2, gw1, gw2, core_in, got,
     x_in, cot_in, stage, vec, gvec, vin, gin, narrow_rows,
     at, n1, q6, k6, v6, o6, pt, h1, acc, n2, act, gp, ta, tb, tc, d6,
     w1_other, w2_other, n2_other, cot_other, back_in, ahead_in,
     lines, b1, gb1, totals, turned1, got1, got2,
     local_sem, ag_send, ag_recv, core_send, core_recv, rs_send, rs_recv,
     a2a_send, a2a_recv, v_send, v_recv, pair_send, pair_recv) = refs

    i = lax.axis_index("blk")
    b = lax.axis_index("batch")
    c, y = lax.rem(i, 2), lax.div(i, 2)
    g, r = lax.div(b, sub), lax.rem(b, sub)
    x, z = lax.rem(g, 2), lax.div(g, 2)

    def device(c_=c, y_=y, x_=x, z_=z):
        return {"blk": 2 * y_ + c_, "batch": (2 * z_ + x_) * sub + r}

    def z_at(k):
        return lax.rem(z + k, zs)

    def block_at(k):
        return lax.rem(i + k, 4)

    def copy(src, dst, send, recv, to):
        return pltpu.make_async_remote_copy(
            src_ref=src, dst_ref=dst, send_sem=send, recv_sem=recv, device_id=to, device_id_type=MESH
        )

    def loop(count, body, hooks=()):
        def step(s, carry):
            body(s)
            for k, f in hooks:
                pl.when(s == k)(f)
            return carry

        lax.fori_loop(0, count, step, 0)

    partners = [device(z_=z_at(k)) for k in range(1, zs)]
    partners += [device(x_=1 - x), device(y_=1 - y), device(c_=1 - c), device(c_=1 - c, y_=1 - y)]
    barrier = pltpu.get_barrier_semaphore()
    for partner in partners:
        pl.semaphore_signal(barrier, inc=1, device_id=partner, device_id_type=MESH)
    pl.semaphore_wait(barrier, len(partners))

    def offsets(axes):
        return [(dy, dx, dz)
                for dy in ((1,) if "y" in axes else (0,))
                for dx in ((1,) if "x" in axes else (0,))
                for dz in (range(1, zs) if "z" in axes else (0,))]

    def owner(d):
        dy, dx, dz = d
        return (1 - y if dy else y, 1 - x if dx else x, z if isinstance(dz, int) and dz == 0 else z_at(zs - dz))

    def moves(d, axis):
        dy, dx, dz = d
        if axis == "y":
            return [(device(y_=1 - y), (1, dx, dz))]
        if axis == "x":
            return [(device(x_=1 - x), (dy, 1, dz))]
        return [(device(z_=z_at(k)), (dy, dx, k)) for k in range(1, zs)]

    def piece(n, d):
        return n.u.at[owner(d) + (n.rows,)]

    def ag_copy(n, ref, d, to):
        slot = (d[0] * 2 + d[1]) * zs + d[2]
        return copy(ref, ref, ag_send.at[n.index, slot], ag_recv.at[n.index, slot], to)

    def core_copy(n, ref):
        return copy(ref, ref, core_send.at[n.index], core_recv.at[n.index], device(c_=1 - c))

    def ag_send_part(n, axes, axis):
        for d in offsets(axes):
            ref = piece(n, d)
            for to, there in moves(d, axis):
                ag_copy(n, ref, there, to).start()

    def ag_wait_part(n, axes):
        for d in offsets(axes):
            ref = piece(n, d)
            ag_copy(n, ref, d, device()).wait_recv()
            if n.other is not None:
                core_copy(n, ref).start()

    def ag_done(n):
        if n.other is not None:
            core_copy(n, n.other.at[:, :, :, n.rows]).wait_recv()

    def ag_drain(n):
        own = piece(n, (0, 0, 0))
        for d in [(dy, dx, dz) for dy in range(2) for dx in range(2) for dz in range(zs)][1:]:
            ag_copy(n, own, d, device()).wait_send()
        if n.other is not None:
            core_copy(n, n.u.at[:, :, :, n.rows]).wait_send()

    AXES = "yxz"

    def step_region(n, step, k):
        where = []
        for axis in AXES:
            at_step = n.route.index(axis)
            where.append(0 if at_step < step else (k if at_step == step else slice(None)))
        return n.got.at[tuple(where) + (n.rows,)]

    def step_groups(n, step):
        axis = n.route[step]
        if axis == "y":
            return [(1, 0, device(y_=1 - y))]
        if axis == "x":
            return [(1, 1, device(x_=1 - x))]
        return [(k, 1 + k, device(z_=z_at(zs - k))) for k in range(1, zs)]

    def rs_group(n, step, k, slot, to):
        ref = step_region(n, step, k)
        return copy(ref, ref, rs_send.at[n.index, slot], rs_recv.at[n.index, slot], to)

    def step_offsets(n, step, k):
        spans = []
        for axis, size in zip(AXES, (2, 2, zs)):
            at_step = n.route.index(axis)
            spans.append((0,) if at_step < step else ((k,) if at_step == step else tuple(range(size))))
        return spans

    def add_terms(n, d, step):
        dy, dx, dz = d
        value = piece(n, d)[...].astype(F32)
        if n.other is not None:
            value = value + n.core_in[dy, dx, dz, n.rows].astype(F32)
        for axis in n.route[:step]:
            if axis == "y":
                value = value + n.got[1, dx, dz, n.rows].astype(F32)
            elif axis == "x":
                value = value + n.got[dy, 1, dz, n.rows].astype(F32)
            else:
                for k in range(1, zs):
                    value = value + n.got[dy, dx, k, n.rows].astype(F32)
        return value

    def rs_start(n):
        for dy in range(2):
            for dx in range(2):
                for dz in range(zs):
                    d = (dy, dx, dz)
                    copy(n.other.at[owner(d) + (n.rows,)], n.core_in.at[d + (n.rows,)], rs_send.at[n.index, zs + 1],
                         rs_recv.at[n.index, zs + 1], device(c_=1 - c)).start()

    def rs_core_whole(n):
        ref = n.core_in.at[:, :, :, n.rows]
        return copy(ref, ref, rs_send.at[n.index, zs + 1], rs_recv.at[n.index, zs + 1], device(c_=1 - c))

    def rs_step(n, step):
        if step == 0 and n.other is not None:
            rs_core_whole(n).wait_recv()
        if step > 0:
            for k, slot, to in step_groups(n, step - 1):
                rs_group(n, step - 1, k, slot, to).wait_recv()
        if step == 3:
            n.total[n.rows, :] = add_terms(n, (0, 0, 0), 3)
            return
        for k, slot, to in step_groups(n, step):
            dys, dxs, dzs = step_offsets(n, step, k)
            if step > 0 or n.other is not None:

                def body(e):
                    for dy in dys:
                        for dx in dxs:
                            d = (dy, dx, dzs[0] if len(dzs) == 1 else e)
                            piece(n, d)[...] = add_terms(n, d, step).astype(BF16)

                if len(dzs) == 1:
                    body(0)
                else:
                    loop(zs, body)
            for dy in dys:
                for dx in dxs:
                    for dz in dzs:
                        d = (dy, dx, dz)
                        copy(piece(n, d), n.got.at[d + (n.rows,)], rs_send.at[n.index, slot],
                             rs_recv.at[n.index, slot], to).start()

    def rs_drain(n):
        if n.other is not None:
            rs_core_whole(n).wait_send()
        for step in range(3):
            for group in step_groups(n, step):
                rs_group(n, step, *group).wait_send()

    def small_sum(ref, slots, which):
        to = (device(y_=1 - y), device(c_=1 - c), device(x_=1 - x))
        to += tuple(device(z_=z_at(k)) for k in range(1, zs))

        def moved(slot):
            return copy(ref, slots.at[slot], v_send.at[which, slot], v_recv.at[which, slot], to[slot])

        def land(last):
            moved(last).wait()
            ref[...] = ref[...] + slots[last]

        def step(n):
            def run():
                if n > 0:
                    land(n - 1)
                moved(n).start()

            return run

        def line():
            land(2)
            for k in range(1, zs):
                moved(2 + k).start()

        def finish():
            for k in range(1, zs):
                moved(2 + k).wait()
            value = ref[...]
            for k in range(1, zs):
                value = value + slots[2 + k]
            ref[...] = value

        return [step(0), step(1), step(2), line, finish]

    def rows_of(s):
        return pl.ds(pl.multiple_of(s * 128, 128), 128)

    def exchange(src, dst, which):
        return [copy(src.at[block_at(k)], dst.at[i], a2a_send.at[which, k - 1],
                     a2a_recv.at[which, k - 1], {"blk": block_at(k), "batch": b})
                for k in range(1, 4)]

    def exchange_landed(dst, which):
        return [copy(dst.at[block_at(4 - k)], dst.at[block_at(4 - k)], a2a_send.at[which, k - 1],
                     a2a_recv.at[which, k - 1], {"blk": block_at(4 - k), "batch": b})
                for k in range(1, 4)]

    def axes_of(mask):
        return "".join(axis for axis, bit in (("y", Y), ("x", X), ("z", Z)) if mask & bit)

    def rows_in(part, count):
        return pl.ds(part * (288 // count), 288 // count)

    units = []
    for unit, routes in enumerate(GATHER_ROUTES):
        half = unit % 2
        ref = (ua, uw1, uw2)[unit // 2]
        pieces = (ref.at[half, c], ref.at[half, 1 - c]) if unit < 2 else (ref.at[half], None)
        for part, route in enumerate(routes):
            units.append(Unit(len(units), "".join(map(axes_of, route)), rows_in(part, len(routes)), *pieces))

    def pair(slot, src, dst):
        return copy(src, dst, pair_send.at[slot], pair_recv.at[slot], device(c_=1 - c))

    w1_swap, w2_swap = pair(0, w1_in, w1_other), pair(1, w2_in, w2_other)

    def each_core(f):
        for q in range(2):
            pl.when(c == q)(functools.partial(f, q))

    def rest_rows(matrix):
        return a_in[matrix, pl.ds(pl.multiple_of(128 * (1 - c), 64), 64), :]

    def own_attention(p):
        mine = ua.at[p, c, y, x, z]
        for m in range(2):
            main = a_in[2 * p + m, pl.ds(pl.multiple_of(64 * c, 64), 128), :]
            mine[96 * m : 96 * m + 96, :] = main.T.astype(BF16)
        rest = jnp.concatenate([rest_rows(2 * p + c), rest_rows(2 * p + 1 - c)], axis=0)
        mine[192:288, :] = rest.T.astype(BF16)

    def own_expand(q):
        both = (w1_in, w1_other) if q == 0 else (w1_other, w1_in)
        cols = slice(192 * q, 192 * q + 192)
        blocks = (
            both[0][0:128, cols],
            jnp.concatenate([both[0][128:192, cols], both[1][0:64, cols]], axis=0),
            both[1][64:192, cols],
        )
        for t, block in enumerate(blocks):
            value = block.T.astype(BF16)
            for h in range(2):
                uw1[h, y, x, z, 96 * t : 96 * t + 96, :] = value[96 * h : 96 * h + 96, :]

    def own_reduce(q):
        both = (w2_in, w2_other) if q == 0 else (w2_other, w2_in)
        for cc in range(2):
            for part_of in range(2):
                start = 384 * part_of + 192 * q
                lines[:, 192 * part_of : 192 * part_of + 192] = both[cc][:, start : start + 192]
            for t in range(3):
                uw2[cc, y, x, z, 96 * t : 96 * t + 96, :] = lines[:, 128 * t : 128 * t + 128].astype(BF16)

    def own_hidden_bias(q):
        for zz in range(zs):
            for xx in range(2):
                col = 384 * (zz % 2) + 192 * xx
                start = 384 * xx + 192 * q
                b1[zz // 2 : zz // 2 + 1, col : col + 192] = vec[8 + zz : 9 + zz, start : start + 192]

    def hidden_bias_gradient(q):
        for zz in range(zs):
            for xx in range(2):
                col = 384 * (zz % 2) + 192 * xx
                start = 384 * xx + 192 * q
                gvec[8 + zz : 9 + zz, start : start + 192] = gb1[zz // 2 : zz // 2 + 1, col : col + 192]

    columns = a_in.shape[2]
    placed = lax.broadcasted_iota(jnp.int32, (columns, 768), 1) == (
        lax.broadcasted_iota(jnp.int32, (columns, 768), 0) + columns * g
    )

    def own_vectors():
        vec[...] = jnp.zeros_like(vec)
        rows = dot_nn(vec_in[...].astype(BF16), jnp.where(placed, 1.0, 0.0).astype(BF16))
        for j in range(3):
            vec[pl.ds(3 * i + j, 1), :] = rows[j : j + 1, :]

    load_cot = pltpu.make_async_copy(cot, stage, local_sem.at[4])

    def masked_cotangent():
        load_cot.wait()
        eye = lax.broadcasted_iota(jnp.int32, (128, 128), 0) == lax.broadcasted_iota(jnp.int32, (128, 128), 1)
        for s in range(4):
            row = jnp.broadcast_to(mask_in[s : s + 1, :].astype(F32), (128, 128))
            column = jnp.sum(jnp.where(eye, row, 0.0), axis=1, keepdims=True)
            stage[s] = (stage[s].astype(F32) * column).astype(BF16)

    def finish_attention(p):
        value = totals.at[p]
        for m in range(2):
            ga[2 * p + m, pl.ds(pl.multiple_of(64 * c, 64), 128), :] = value[96 * m : 96 * m + 96, :].T
        rest = value[192:288, :].T
        rows = pl.ds(pl.multiple_of(128 * (1 - c), 64), 64)
        ga[2 * p + c, rows, :] = rest[0:64, :]
        ga[2 * p + 1 - c, rows, :] = rest[64:128, :]

    w1_back = pair(6, turned1.at[pl.ds(pl.multiple_of(192 * (1 - c), 64), 192)], got1)
    w2_back = pair(7, totals.at[5 - c], got2)

    def turn_expand():
        for h in range(2):
            for t in range(3):
                turned1[128 * t : 128 * t + 128, 96 * h : 96 * h + 96] = totals[2 + h, 96 * t : 96 * t + 96, :].T
        w1_back.start()

    def join_expand(q):
        g1[:, 192 * q : 192 * q + 192] = turned1[192 * q : 192 * q + 192, :]
        g1[:, 192 * (1 - q) : 192 * (1 - q) + 192] = got1[...]

    def join_reduce(q):
        for half, value in ((q, totals.at[4 + q]), (1 - q, got2)):
            for t in range(3):
                lines[:, 128 * t : 128 * t + 128] = value[96 * t : 96 * t + 96, :]
            for part_of in range(2):
                start = 384 * part_of + 192 * half
                g2[:, start : start + 192] = lines[:, 192 * part_of : 192 * part_of + 192]

    def finish_vectors():
        value, total = gvec[...], 0.0
        for _ in range(3):
            part = value.astype(BF16)
            total = total + dot_nt(part, jnp.where(placed, 1.0, 0.0).astype(BF16))
            value = value - part.astype(F32)
        narrow_rows[...] = total
        for j in range(3):
            gv[j : j + 1, :] = narrow_rows[pl.ds(3 * i + j, 1), :]

    grads, owners = [], []
    for unit, routes in enumerate(SUM_ROUTES):
        half = unit % 2
        ref = (ua, gw1, gw2)[unit // 2]
        pieces = (ref.at[half, c], ref.at[half, 1 - c], core_in.at[half]) if unit < 2 else (ref.at[half], None, None)
        for part, route in enumerate(routes):
            grads.append(Gradient(len(grads), "".join(map(axes_of, route)), rows_in(part, len(routes)), *pieces,
                                  got.at[unit], totals.at[unit]))
            owners.append(unit)

    def summed(unit):
        if unit < 2:
            finish_attention(unit)
        elif unit < 4 and {2, 3} <= set(whole):
            turn_expand()
        elif unit >= 4 and {4, 5} <= set(whole):
            w2_back.start()

    seen, whole = set(), []

    def event(kind, *rest):
        if kind == SEND:
            ag_send_part(units[rest[0]], axes_of(rest[1]), axes_of(rest[2]))
        elif kind == GOT:
            ag_wait_part(units[rest[0]], axes_of(rest[1]))
        elif kind == WHOLE:
            ag_done(units[rest[0]])
        elif kind == SUM:
            rs_step(grads[rest[0]], rest[1])
            if rest[1] == 3:
                seen.add(rest[0])
                unit = owners[rest[0]]
                if all(k in seen for k in range(len(grads)) if owners[k] == unit):
                    whole.append(unit)
                    summed(unit)
        elif kind == DO:
            actions[rest[0]]()
        else:
            (vec_steps if kind == VEC else gvec_steps)[rest[0] + 1]()

    def run(part):
        for todo in PLAN.get(part, ()):
            event(*todo)

    def parts(name, count, body):
        run(name + "0")
        hooks = [(k - 1, functools.partial(run, name + str(k))) for k in range(1, count) if name + str(k) in PLAN]
        loop(count, body, hooks)

    def started(copies):
        for moved in copies:
            moved.start()
        return copies

    def arrived(*copies):
        for moved in copies:
            moved.wait_recv()

    load_cot.start()
    own_tokens = pltpu.make_async_copy(tok.at[i], x_in.at[i], local_sem.at[0])
    own_tokens.start()
    own_cot = pltpu.make_async_copy(stage.at[i], cot_in.at[i], local_sem.at[1])
    tokens_out, cot_out = exchange(tok, x_in, 0), exchange(stage, cot_in, 1)
    result_out = exchange(stage, out, 2)
    grad_out = [copy(n1.at[rows_of(block_at(k))], ig.at[i], a2a_send.at[3, k - 1], a2a_recv.at[3, k - 1],
                     {"blk": block_at(k), "batch": b}) for k in range(1, 4)]
    own_out = pltpu.make_async_copy(stage.at[i], out.at[i], local_sem.at[2])
    own_grad = pltpu.make_async_copy(n1.at[rows_of(i)], ig.at[i], local_sem.at[3])
    n2_swap, cot_swap = pair(2, n2, n2_other), pair(3, cot_in, cot_other)
    back_swap, ahead_swap = pair(4, d6, back_in), pair(5, n2, ahead_in)
    vec_steps, gvec_steps = small_sum(vec, vin, 0), small_sum(gvec, gin, 1)

    def tokens_here():
        arrived(*exchange_landed(x_in, 0))
        own_tokens.wait()

    def cotangent_here():
        arrived(*exchange_landed(cot_in, 1))
        own_cot.wait()
        cot_swap.start()

    def swaps_here():
        w1_swap.wait()
        w2_swap.wait()

    actions = {
        TOK: lambda: started(tokens_out),
        COT: lambda: started(cot_out),
        OUT: lambda: started(result_out),
        IG: lambda: started(grad_out),
        TOK_HERE: tokens_here,
        COT_HERE: cotangent_here,
        OUT_HERE: lambda: arrived(*exchange_landed(out, 2)),
        IG_HERE: lambda: arrived(*exchange_landed(ig, 3)),
        SWAP_HERE: swaps_here,
        N2S_HERE: lambda: n2_swap.wait(),
        COTS_HERE: lambda: cot_swap.wait(),
        BACKS_HERE: lambda: back_swap.wait(),
        AHEADS_HERE: lambda: ahead_swap.wait(),
    }

    def core_own(first, last):
        for n in units[first : last + 1]:
            core_copy(n, piece(n, (0, 0, 0))).start()

    own_attention(0)
    core_own(*QK)
    w1_swap.start()
    w2_swap.start()
    own_vectors()
    vec_steps[0]()
    run("own1")
    own_attention(1)
    core_own(*VO)
    run("ownff")
    each_core(own_expand)
    each_core(own_reduce)
    run("mask")
    masked_cotangent()
    own_cot.start()
    run("ln1")
    each_core(own_hidden_bias)

    def normalise(value):
        centered = value - jnp.mean(value, axis=-1, keepdims=True)
        scale = lax.rsqrt(jnp.mean(centered * centered, axis=-1, keepdims=True) + norm_epsilon)
        return centered * scale, scale

    def first_norm(s):
        unit, _ = normalise(x_in[s].astype(F32))
        n1[rows_of(s), :] = (unit * vec[0:1, :] + vec[1:2, :]).astype(BF16)

    loop(4, first_norm)
    run("unp0")

    lanes = lax.broadcasted_iota(jnp.int32, (96, 128), 1)

    def unpack(p, s):
        for xx in range(2):
            rows = pl.ds(pl.multiple_of((2 * s + xx) * 96, 96), 96)
            for yy in range(2):
                first, second = ua.at[p, 0, yy, xx, s], ua.at[p, 1, yy, xx, s]
                lo, hi = 384 * yy, 384 * yy + 256
                for m in range(2):
                    at[2 * p + m, rows, lo : lo + 128] = first[96 * m : 96 * m + 96, :]
                    at[2 * p + m, rows, hi : hi + 128] = second[96 * m : 96 * m + 96, :]
                rest_first = first[192:288, :].astype(F32)
                rest_second = second[192:288, :].astype(F32)
                even = jnp.where(lanes < 64, rest_first, rest_second)
                odd = pltpu.roll(jnp.where(lanes < 64, rest_second, rest_first), 64, 1)
                at[2 * p, rows, lo + 128 : lo + 256] = even.astype(BF16)
                at[2 * p + 1, rows, lo + 128 : lo + 256] = odd.astype(BF16)

    def project(m, dst, bias):
        for n in range(3):
            value = dot_nt(n1[...], at[m, 256 * n : 256 * n + 256, :])
            if bias is not None:
                value = value + vec[bias : bias + 1, 256 * n : 256 * n + 256]
            value = value.astype(BF16)
            if m == 0:
                value = value * jnp.asarray(HEAD ** (-0.5), BF16)
            dst[2 * n] = value[:, 0:128]
            dst[2 * n + 1] = value[:, 128:256]

    loop(zs, functools.partial(unpack, 0))
    run("projq")
    project(0, q6, 2)
    run("projk")
    project(1, k6, None)

    half_lane = lax.broadcasted_iota(jnp.int32, (512, 128), 1) // HEAD

    def half_of(value, which):
        return jnp.where(half_lane == which, value, jnp.zeros_like(value))

    def turn(value):
        return value.astype(F32).T.astype(BF16)

    def attend(p):
        queries, keys = q6[p], k6[p]
        for which in range(2):
            scores = dot_nt(half_of(keys, which), queries)
            expo = jnp.exp(scores - jnp.max(scores, axis=0, keepdims=True))
            probs = (expo * (1.0 / jnp.sum(expo, axis=0, keepdims=True))).astype(BF16)
            pt[2 * p + which] = probs

    def mix(p):
        values_t = turn(v6[p])
        mixed = [dot_nn(values_t[64 * which : 64 * which + 64, :], pt[2 * p + which]) for which in range(2)]
        o6[p] = jnp.concatenate(mixed, axis=0).T.astype(BF16)

    parts("attend", 6, attend)
    run("unp1")
    loop(zs, functools.partial(unpack, 1))
    run("projv")
    project(2, v6, 3)
    parts("mix", 6, mix)

    run("ao")
    for n in range(3):
        cols = slice(256 * n, 256 * n + 256)
        value = dot_nt(lane_tiles(o6), at[3, cols, :]) + vec[4:5, cols]
        for s in range(4):
            h1[128 * s : 128 * s + 128, cols] = x_in[s, :, cols].astype(F32) + value[128 * s : 128 * s + 128]

    def second_norm(s):
        unit, _ = normalise(h1[rows_of(s), :])
        n2[rows_of(s), :] = (unit * vec[5:6, :] + vec[6:7, :]).astype(BF16)

    run("ln2")
    loop(4, second_norm)
    n2_swap.start()

    def expand_block(s):
        def piece(ref):
            return jnp.concatenate([ref[96 * t : 96 * t + 96, :] for t in range(3)], axis=1)

        return jnp.concatenate(
            [jnp.concatenate([piece(uw1.at[h, yy, xx, 2 * s + zz]) for yy in range(2)], axis=1)
             for zz in range(2) for xx in range(2) for h in range(2)],
            axis=0,
        )

    def reduce_block(s):
        def piece(ref):
            return jnp.concatenate([ref[96 * t : 96 * t + 96, :] for t in range(3)], axis=1)

        return jnp.concatenate(
            [jnp.concatenate([piece(uw2.at[cc, s, xx, zz]) for cc in range(2)], axis=1)
             for zz in range(zs) for xx in range(2)],
            axis=0,
        )

    def block_rows(owner, s):
        return pl.ds(pl.multiple_of((2 * owner + s) * 512, 512), 512)

    def expand(owner, normed, s):
        rows = block_rows(owner, s)
        inner = dot_nt(normed[...], expand_block(s)) + b1[pl.ds(s, 1), :]
        square = inner * inner
        tanh = jnp.tanh(GELU_SCALE * inner * (1.0 + GELU_CUBE * square))
        act[rows, :] = (0.5 * inner * (1.0 + tanh)).astype(BF16)
        slope = 0.5 * (1.0 + tanh) + 0.5 * inner * (1.0 - tanh * tanh) * (
            GELU_SCALE * (1.0 + 3.0 * GELU_CUBE * square)
        )
        gp[rows, :] = slope.astype(BF16)

    parts("expa", 2, functools.partial(expand, 0, n2))
    parts("expb", 2, functools.partial(expand, 1, n2_other))

    gvec[...] = jnp.zeros_like(gvec)

    def transpose_rows(dst, s, value):
        dst[:, 128 * s : 128 * s + 128] = turn(value)

    run("trY")
    total = jnp.zeros((1, 768), F32)
    for s in range(4):
        transpose_rows(ta, s, cot_in[s])
        total = total + jnp.sum(cot_in[s].astype(F32), axis=0, keepdims=True)
    gvec[7:8, :] = total
    for s in range(4):
        transpose_rows(tb, s, cot_other[s])

    def both_rows(ref, s):
        return jnp.concatenate([ref[block_rows(0, s), :], ref[block_rows(1, s), :]], axis=0)

    def reduce_back(s):
        grad = dot_nn(jnp.concatenate([ta[...], tb[...]], axis=1), both_rows(act, s)).astype(BF16)
        for zz in range(zs):
            for xx in range(2):
                row = 96 * (2 * zz + xx)
                for cc in range(2):
                    for t in range(3):
                        col = 384 * cc + 128 * t
                        gw2[cc, s, xx, zz, 96 * t : 96 * t + 96, :] = grad[row : row + 96, col : col + 128]

    parts("gw2_", 2, reduce_back)

    def rows_together(ref):
        return jnp.concatenate([ref[s] for s in range(4)], axis=0)

    def inner_back(owner, cotangent_rows, s):
        rows = block_rows(owner, s)
        grad = dot_nn(rows_together(cotangent_rows), reduce_block(s)) * gp[rows, :].astype(F32)
        low = grad.astype(BF16)
        gp[rows, :] = low
        sums = jnp.sum(low.astype(F32), axis=0, keepdims=True)
        gb1[pl.ds(s, 1), :] = sums if owner == 1 else gb1[pl.ds(s, 1), :] + sums

    def norm_back(owner):
        acc[...] = dot_nn(gp[block_rows(owner, 0), :], expand_block(0))
        acc[...] += dot_nn(gp[block_rows(owner, 1), :], expand_block(1))

    parts("innb", 2, functools.partial(inner_back, 1, cot_other))
    run("dn2b")
    norm_back(1)
    for t in range(6):
        d6[t] = acc[:, 128 * t : 128 * t + 128].astype(BF16)
    back_swap.start()
    parts("inna", 2, functools.partial(inner_back, 0, cot_in))
    each_core(hidden_bias_gradient)
    run("dn2a")
    norm_back(0)

    def expand_back(s):
        turned = jnp.concatenate([turn(gp[block_rows(owner, s), :]) for owner in range(2)], axis=1)
        normed = jnp.concatenate([n2[...], n2_other[...]], axis=0)
        grad = dot_nn(turned, normed).astype(BF16)
        for zz in range(2):
            for xx in range(2):
                for h in range(2):
                    row = 384 * zz + 192 * xx + 96 * h
                    for yy in range(2):
                        for t in range(3):
                            col = 384 * yy + 128 * t
                            gw1[h, yy, xx, 2 * s + zz, 96 * t : 96 * t + 96, :] = grad[
                                row : row + 96, col : col + 128
                            ]

    parts("gw1_", 2, expand_back)
    run("hid")

    def norm_gradient(value, scale_row, grad):
        unit, scale = normalise(value)
        gain_sum = jnp.sum(grad * unit, axis=0, keepdims=True)
        bias_sum = jnp.sum(grad, axis=0, keepdims=True)
        inner = grad * scale_row
        mean = jnp.mean(inner, axis=-1, keepdims=True)
        along = jnp.mean(inner * unit, axis=-1, keepdims=True)
        return scale * (inner - mean - unit * along), gain_sum, bias_sum

    def hidden_back(s):
        rows = rows_of(s)
        grad_in = jnp.concatenate([back_in[t, rows, :] for t in range(6)], axis=1)
        grad_in = acc[rows, :] + grad_in.astype(F32)
        grad, gain_sum, bias_sum = norm_gradient(h1[rows, :], vec[5:6, :], grad_in)
        grad = grad + cot_in[s].astype(F32)
        acc[rows, :] = grad
        low = grad.astype(BF16)
        n2[rows, :] = low
        gvec[5:6, :] += gain_sum
        gvec[6:7, :] += bias_sum
        gvec[4:5, :] += jnp.sum(low.astype(F32), axis=0, keepdims=True)

    loop(4, hidden_back)

    run("dO")
    for n in range(3):
        value = dot_nn(n2[...], at[3, :, 256 * n : 256 * n + 256]).astype(BF16)
        d6[2 * n] = value[:, 0:128]
        d6[2 * n + 1] = value[:, 128:256]
    run("gao")
    for s in range(4):
        transpose_rows(tc, s, n2[128 * s : 128 * s + 128, :])
    gp[768:1536, :] = dot_nn(tc[...], lane_tiles(o6)).astype(BF16)

    def attend_back(p):
        rows = rows_of(p)
        queries, keys, values, grads_in = q6[p], k6[p], v6[p], d6[p]
        keys_t = turn(keys)
        grad_query, grad_key, grad_value = [], 0.0, 0.0
        for which in range(2):
            probs = pt[2 * p + which]
            wide = probs.astype(F32)
            grad_probs = dot_nt(half_of(values, which), grads_in)
            inner = jnp.sum(wide * grad_probs, axis=0, keepdims=True)
            grad_scores = (wide * (grad_probs - inner)).astype(BF16)
            grad_query.append(dot_nn(keys_t[64 * which : 64 * which + 64, :], grad_scores))
            grad_key = grad_key + dot_nn(grad_scores, half_of(queries, which))
            grad_value = grad_value + dot_nn(probs, half_of(grads_in, which))
        grad_query = jnp.concatenate(grad_query, axis=0) * HEAD ** (-0.5)
        ta[rows, :] = grad_query.astype(BF16)
        tb[rows, :] = grad_key.T.astype(BF16)
        tc[rows, :] = grad_value.T.astype(BF16)
        q6[p] = grad_query.T.astype(BF16)
        k6[p] = grad_key.astype(BF16)
        v6[p] = grad_value.astype(BF16)

    def pack(p, first_row, second_row):
        def body(s):
            for xx in range(2):
                offset = (2 * s + xx) * 96
                rows = [pl.ds(pl.multiple_of(first_row + offset, 96), 96),
                        pl.ds(pl.multiple_of(second_row + offset, 96), 96)]
                first, second = ua.at[p, 0, :, xx, s], ua.at[p, 1, :, xx, s]
                for yy in range(2):
                    lo, mid, hi = 384 * yy, 384 * yy + 128, 384 * yy + 256
                    for m in range(2):
                        first[yy, 96 * m : 96 * m + 96, :] = gp[rows[m], lo : lo + 128]
                        second[yy, 96 * m : 96 * m + 96, :] = gp[rows[m], hi : hi + 128]
                    even = gp[rows[0], mid : mid + 128].astype(F32)
                    odd = pltpu.roll(gp[rows[1], mid : mid + 128].astype(F32), 64, 1)
                    first[yy, 192:288, :] = jnp.where(lanes < 64, even, odd).astype(BF16)
                    second[yy, 192:288, :] = jnp.where(lanes < 64, odd, even).astype(BF16)

        loop(zs, body)

    parts("ab", 6, attend_back)
    run("gav")
    for n in units[VO[0] : VO[1] + 1]:
        ag_drain(n)
    gp[0:768, :] = dot_nn(tc[...], n1[...]).astype(BF16)
    pack(1, 0, 768)
    for n in grads[AVO[0] : AVO[1] + 1]:
        rs_start(n)
    run("gaqk")
    for n in units[QK[0] : QK[1] + 1]:
        ag_drain(n)
    gp[0:768, :] = dot_nn(ta[...], n1[...]).astype(BF16)
    gp[768:1536, :] = dot_nn(tb[...], n1[...]).astype(BF16)
    pack(0, 0, 768)
    for n in grads[AQK[0] : AQK[1] + 1]:
        rs_start(n)

    def reduce(owner):
        value = dot_nt(act[block_rows(owner, 0), :], reduce_block(0))
        return value + dot_nt(act[block_rows(owner, 1), :], reduce_block(1))

    def layer_output():
        run("redb")
        n2[...] = reduce(1).astype(BF16)
        ahead_swap.start()
        run("reda")
        h1[...] = h1[...] + vec[7:8, :] + reduce(0)
        run("outst")
        for moved in cot_out:
            moved.wait_send()
        for s in range(4):
            rows = slice(128 * s, 128 * s + 128)
            stage[s] = (h1[rows, :] + ahead_in[rows, :].astype(F32)).astype(BF16)
        own_out.start()

    layer_output()
    run("dn1")
    h1[...] = dot_nn(lane_tiles(q6), at[0])
    h1[...] += dot_nn(lane_tiles(k6), at[1])
    h1[...] += dot_nn(lane_tiles(v6), at[2])
    gvec[2:3, :] = jnp.sum(lane_tiles(q6).astype(F32), axis=0, keepdims=True)
    gvec[3:4, :] = jnp.sum(lane_tiles(v6).astype(F32), axis=0, keepdims=True)

    run("inb")

    def input_back(s):
        rows = rows_of(s)
        grad, gain_sum, bias_sum = norm_gradient(x_in[s].astype(F32), vec[0:1, :], h1[rows, :])
        n1[rows, :] = (grad + acc[rows, :]).astype(BF16)
        gvec[0:1, :] += gain_sum
        gvec[1:2, :] += bias_sum

    loop(4, input_back)
    gvec_steps[0]()
    own_grad.start()
    run("end")
    finish_vectors()
    w1_back.wait()
    each_core(join_expand)
    w2_back.wait()
    each_core(join_reduce)

    own_out.wait()
    own_grad.wait()
    for moved in tokens_out + result_out + grad_out:
        moved.wait_send()
    for n in units[VO[1] + 1 :]:
        ag_drain(n)
    for n in grads:
        rs_drain(n)


def layer(sub, tokens, cotangent, span_mask, vectors, attention, expand, reduce_t):
    zs = GROUPS // 2
    seqs, block, width = tokens.shape
    rows = seqs * block
    columns = attention.shape[2]
    piece = (3 * columns, 128)
    vmem = lambda shape, dtype: pltpu.VMEM(shape, dtype)
    half = (2, 2, 2, zs) + piece
    scratch = [vmem((2,) + half, BF16)] + [vmem(half, BF16)] * 4
    scratch += [vmem((2, 2, 2, zs) + piece, BF16), vmem((6, 2, 2, zs) + piece, BF16)]
    scratch += [vmem(tokens.shape, BF16)] * 3
    scratch += [vmem((16, width), F32)] * 2
    scratch += [vmem((zs + 2, 16, width), F32)] * 2
    scratch += [vmem((16, columns), F32)]
    tiles = vmem((width // 128, rows, 128), BF16)
    flat = vmem((rows, width), BF16)
    turned = vmem((width, rows), BF16)
    scratch += [vmem((4, width, width), BF16), flat, tiles, tiles, tiles, tiles]
    scratch += [vmem((HEADS, rows, rows), BF16), vmem((rows, width), F32), vmem((rows, width), F32)]
    scratch += [flat, vmem((4 * rows, width), BF16), vmem((4 * rows, width), BF16)]
    scratch += [turned, turned, turned, tiles]
    scratch += [vmem(expand.shape, F32), vmem(reduce_t.shape, F32), flat, vmem(tokens.shape, BF16)]
    scratch += [tiles, flat, vmem((columns, width // 2), F32), vmem((2, width), F32), vmem((2, width), F32)]
    scratch += [vmem((6,) + piece, F32), vmem((width // 2, 2 * columns), F32)]
    scratch += [vmem((2 * columns, 2 * columns), F32), vmem(piece, F32)]
    scratch += [pltpu.SemaphoreType.DMA((5,))]
    gathered, summed = sum(map(len, GATHER_ROUTES)), sum(map(len, SUM_ROUTES))
    scratch += [pltpu.SemaphoreType.DMA((gathered, 4 * zs))] * 2
    scratch += [pltpu.SemaphoreType.DMA((gathered,))] * 2
    scratch += [pltpu.SemaphoreType.DMA((summed, zs + 2))] * 2
    scratch += [pltpu.SemaphoreType.DMA((4, 3))] * 2
    scratch += [pltpu.SemaphoreType.DMA((2, zs + 2))] * 2
    scratch += [pltpu.SemaphoreType.DMA((8,))] * 2
    in_vmem = pl.BlockSpec(memory_space=pltpu.VMEM)
    anywhere = pl.BlockSpec(memory_space=pl.ANY)
    return pl.pallas_call(
        functools.partial(kernel, sub, zs),
        out_shape=(
            jax.ShapeDtypeStruct(tokens.shape, BF16),
            jax.ShapeDtypeStruct(tokens.shape, BF16),
            jax.ShapeDtypeStruct(attention.shape, F32),
            jax.ShapeDtypeStruct(expand.shape, F32),
            jax.ShapeDtypeStruct(reduce_t.shape, F32),
            jax.ShapeDtypeStruct(vectors.shape, F32),
        ),
        in_specs=[anywhere] * 2 + [in_vmem] * 5,
        out_specs=(anywhere, anywhere) + (in_vmem,) * 4,
        scratch_shapes=scratch,
        compiler_params=pltpu.CompilerParams(
            collective_id=0, has_side_effects=True, vmem_limit_bytes=65400 * 1024
        ),
    )(tokens, cotangent, span_mask, vectors, attention, expand, reduce_t)


def update_kernel(rates, *refs):
    count = len(rates)
    ins, (result, grad) = refs[: 4 * count], refs[4 * count : 4 * count + 2]
    outs, (result_out, grad_out) = refs[4 * count + 2 : 7 * count + 2], refs[7 * count + 2 : 7 * count + 4]
    held, (low, wide, passed) = refs[7 * count + 4 : 11 * count + 4], refs[11 * count + 4 : 11 * count + 7]
    in_sems, out_sems = refs[11 * count + 7 :]
    loads = [pltpu.make_async_copy(ins[n], held[n], in_sems.at[n]) for n in range(4 * count)]
    stores = [pltpu.make_async_copy(held[4 * n + m], outs[3 * n + m], out_sems.at[3 * n + m])
              for n in range(count) for m in range(3)]
    load_grad = pltpu.make_async_copy(grad, low, in_sems.at[4 * count])
    store_grad = pltpu.make_async_copy(wide, grad_out, out_sems.at[3 * count])
    load_result = pltpu.make_async_copy(result, passed, in_sems.at[4 * count + 1])
    store_result = pltpu.make_async_copy(passed, result_out, out_sems.at[3 * count + 1])
    load_grad.start()
    load_result.start()
    for copy in loads:
        copy.start()
    load_result.wait()
    store_result.start()
    load_grad.wait()

    def widen(s, carry):
        wide[s] = low[s].astype(F32)
        return carry

    lax.fori_loop(0, low.shape[0], widen, 0)
    store_grad.start()
    for n in range(count):
        for m in range(4):
            loads[4 * n + m].wait()
        weight, one, two, gradient = held[4 * n : 4 * n + 4]
        values = adamw(weight[...], one[...], two[...], gradient[...], rates[n])
        for ref, value in zip((weight, one, two), values):
            ref[...] = value
        for m in range(3):
            stores[3 * n + m].start()
    for copy in stores + [store_grad, store_result]:
        copy.wait()


def update(rates, arrays, result, grad):
    flat = [value for group in arrays for value in group]
    new = [jax.ShapeDtypeStruct(value.shape, F32) for group in arrays for value in group[:3]]
    new += [jax.ShapeDtypeStruct(result.shape, BF16), jax.ShapeDtypeStruct(grad.shape, F32)]
    anywhere = pl.BlockSpec(memory_space=pl.ANY)
    scratch = [pltpu.VMEM(value.shape, F32) for value in flat]
    scratch += [pltpu.VMEM(grad.shape, BF16), pltpu.VMEM(grad.shape, F32), pltpu.VMEM(result.shape, BF16)]
    scratch += [pltpu.SemaphoreType.DMA((len(flat) + 2,)), pltpu.SemaphoreType.DMA((len(new),))]
    return pl.pallas_call(
        functools.partial(update_kernel, rates),
        out_shape=tuple(new),
        in_specs=[anywhere] * (len(flat) + 2),
        out_specs=(anywhere,) * len(new),
        scratch_shapes=scratch,
        compiler_params=pltpu.CompilerParams(vmem_limit_bytes=63 * 1024 * 1024),
    )(*flat, result, grad)


def local(
    sub,
    tokens,
    cotangent,
    span_mask,
    attention_weight,
    expand_weight,
    reduce_weight,
    vectors,
    attention_first,
    attention_second,
    expand_first,
    expand_second,
    reduce_first,
    reduce_second,
    vector_first,
    vector_second,
):
    together = [[n * sub + m for m in range(sub)] for n in range(GROUPS)]

    def widen(value, axis):
        if sub == 1:
            return value
        low = lax.all_gather(
            value.astype(BF16), "batch", axis=axis, tiled=True, axis_index_groups=together
        )
        return low.astype(F32)

    def narrow(value, axis):
        if sub == 1:
            return value
        return lax.psum_scatter(
            value, "batch", scatter_dimension=axis, tiled=True, axis_index_groups=together
        )

    out_tokens, input_grad, ga, g1, g2, gv = layer(
        sub,
        tokens,
        cotangent,
        span_mask,
        widen(vectors, 1),
        widen(attention_weight, 2),
        widen(expand_weight, 1),
        widen(reduce_weight.T, 0),
    )
    arrays = (
        (attention_weight, attention_first, attention_second, narrow(ga, 2)),
        (expand_weight, expand_first, expand_second, narrow(g1, 1)),
        (reduce_weight.T, reduce_first.T, reduce_second.T, narrow(g2, 0)),
        (vectors, vector_first, vector_second, narrow(gv, 1)),
    )
    rates = (rate_attention, rate_expand, rate_reduce, rate_vector)
    new = update(rates, arrays, out_tokens, input_grad)
    return new[-2:] + new[0:6] + tuple(value.T for value in new[6:9]) + new[9:12]


def solution(mesh):
    sub = mesh.shape["batch"] // GROUPS
    sequences = P("batch", "blk", None)
    attention = P(None, "blk", "batch")
    matrix = P("blk", "batch")
    return jax.shard_map(
        functools.partial(local, sub),
        mesh=mesh,
        in_specs=(sequences, sequences, P("batch", "blk"), attention, matrix, matrix, matrix)
        + (attention,) * 2
        + (matrix,) * 6,
        out_specs=(sequences,) * 2 + (attention,) * 3 + (matrix,) * 9,
        check_vma=False,
    )
```

profile of v0, /device:TPU:0, one launch (start us, length us, event | category | flops | bytes accessed | tf_op | source)
XLA Modules:
  0.0 162.3 jit_solution(9286738373520215046)
XLA Ops:
  0.6 156.8 %shard_map.254 = (bf16[4,128,768]{2,1,0:T(8,128)(2,1)}, bf16[4,128,768]{2,1,0:T(8,128)(2,1)}, f32[4,192,96]{2,1,0:T(8,128)}, f32[192,384]{1,0:T(8,128)}, f32[96,768]{1,0:T(8,128)}, /*index=5*/f32[3,96]{1,0:T(4,128)}) custom-call(bf16[4,128,768]{2,1,0:T(8,128)(2,1)} %refs_0_.2, bf16[4,128,768]{2,1,0:T(8,128)(2,1)} %refs_1_.2, s32[4,128]{1,0:T(4,128)} %refs_2_.2, ...), custom_call_target="tpu_custom_call" | custom-call | tf_op jit(solution)/shard_map/pallas_call | solution.py:1108
  157.4 4.7 %shard_map.255 = (f32[4,192,96]{2,1,0:T(8,128)}, f32[4,192,96]{2,1,0:T(8,128)}, f32[4,192,96]{2,1,0:T(8,128)}, f32[192,384]{1,0:T(8,128)}, f32[192,384]{1,0:T(8,...) custom-call(f32[4,192,96]{2,1,0:T(8,128)} %refs_0_.3, ...), custom_call_target="tpu_custom_call" | custom-call | tf_op jit(solution)/shard_map/pallas_call | solution.py:1175
where the time goes:
time: 162 us
  Pallas kernels  161 us (99%)
    pallas_call x1, Pallas kernels, layer(): pl.pallas_call(functools.partial(kernel, sub, zs), out_shape=(jax.ShapeDt...  157 us
    pallas_call x1, Pallas kernels, update(): pl.pallas_call(functools.partial(update_kernel, rates), out_shape=tuple(n...  4.67 us

commit v1 on v0

--- a/solution.py
+++ b/solution.py
@@ -51,167 +51,156 @@
 
 X, Y, Z = 1, 2, 4
 (N_QKA, N_QKB, N_VOA, N_VOB, N_W10A, N_W10B, N_W11A, N_W11B, N_W20A, N_W20B, N_W21A, N_W21B) = range(12)
-(N_AQKA, N_AQKB, N_AVOA, N_AVOB, N_G10, N_G11, N_G20, N_G21) = range(8)
+(N_AQKA, N_AQKB, N_AVO, N_G10, N_G11A, N_G11B, N_G20, N_G21) = range(8)
 QK, VO = (N_QKA, N_QKB), (N_VOA, N_VOB)
-AQK, AVO = (N_AQKA, N_AQKB), (N_AVOA, N_AVOB)
+AQK, AVO = (N_AQKA, N_AQKB), (N_AVO, N_AVO)
 SEND, GOT, WHOLE, SUM, VEC, SMALL, DO = range(7)
 (TOK, COT, OUT, IG, TOK_HERE, COT_HERE, OUT_HERE,
  IG_HERE, SWAP_HERE, N2S_HERE, COTS_HERE, BACKS_HERE, AHEADS_HERE) = range(13)
 GATHER_ROUTES = (
-    ((Z, X, Y), (Z, Y, X),),
     ((Z, Y, X), (Z, Y, X),),
-    ((Y, Z, X), (Y, Z, X),),
-    ((X, Z, Y), (Z, Y, X),),
     ((Z, Y, X), (Z, Y, X),),
-    ((Z, X, Y), (X, Y, Z),),
+    ((Y, Z, X), (X, Z, Y),),
+    ((Z, X, Y), (Y, Z, X),),
+    ((X, Z, Y), (Z, X, Y),),
+    ((Y, Z, X), (Z, Y, X),),
 )
 SUM_ROUTES = (
     ((Y, X, Z), (X, Z, Y),),
-    ((Y, X, Z), (X, Z, Y),),
     ((Y, X, Z),),
-    ((X, Y, Z),),
-    ((Z, Y, X),),
-    ((Y, Z, X),),
+    ((Y, X, Z),),
+    ((X, Z, Y), (X, Z, Y),),
+    ((Y, X, Z),),
+    ((Z, X, Y),),
 )
 PLAN = dict(
     own1=(
-        (SEND, N_QKA, 0, X), (SEND, N_QKA, 0, Z), (SEND, N_QKB, 0, X), (SEND, N_QKB, 0, Y),
-        (SEND, N_QKB, 0, Z),
+        (SEND, N_QKA, 0, Z), (SEND, N_QKB, 0, Z),
     ),
     ownff=(
-        (SEND, N_VOA, 0, X), (SEND, N_VOB, 0, X), (DO, TOK), (SEND, N_VOA, 0, Z), (VEC, 0), (DO, SWAP_HERE),
-        (GOT, N_QKA, X),
+        (DO, TOK), (SEND, N_VOA, 0, Z), (VEC, 0), (DO, SWAP_HERE),
     ),
     mask=(
-        (GOT, N_QKB, Y), (SEND, N_QKB, Y, X), (GOT, N_QKB, X), (SEND, N_W10A, 0, X), (SEND, N_W11A, 0, X),
+        (SEND, N_W10B, 0, X), (SEND, N_W20A, 0, X),
     ),
     ln1=(
-        (GOT, N_VOA, X), (VEC, 1), (GOT, N_QKA, Z), (GOT, N_VOB, X), (SEND, N_QKA, Z, X), (SEND, N_VOB, 0, Z),
-        (GOT, N_QKB, Y | X), (SEND, N_W10B, 0, X), (GOT, N_W11A, X), (VEC, 2), (SEND, N_QKA, Z, Y),
-        (GOT, N_QKB, Z), (SEND, N_QKB, Z, X), (SEND, N_QKB, Z, Y), (SEND, N_W11B, 0, Z), (GOT, N_QKA, Z | X),
-        (SEND, N_W11B, 0, X), (SEND, N_QKA, Z | X, Y), (GOT, N_W10A, X), (GOT, N_VOA, Z), (SEND, N_VOA, Z, X),
-        (DO, TOK_HERE), (SEND, N_W10A, 0, Z), (SEND, N_QKA, 0, Y), (GOT, N_QKB, Z | X), (SEND, N_QKA, X, Y),
-        (GOT, N_W10B, X), (GOT, N_QKB, Z | Y), (SEND, N_QKB, Z | Y, X), (SEND, N_VOA, Z, Y), (GOT, N_VOB, Z),
-        (SEND, N_VOB, Z, X), (VEC, 3), (SEND, N_W10B, 0, Z),
+        (VEC, 1), (GOT, N_QKA, Z), (SEND, N_QKA, Z, X), (SEND, N_QKA, Z, Y), (SEND, N_VOB, 0, Z),
+        (GOT, N_W10B, X), (GOT, N_W20A, X), (GOT, N_QKB, Z), (SEND, N_QKB, Z, X), (SEND, N_QKB, Z, Y),
+        (SEND, N_W11A, 0, Z), (GOT, N_QKA, Z | X), (DO, TOK_HERE), (GOT, N_VOA, Z), (SEND, N_VOA, Z, X),
+        (SEND, N_VOA, Z, Y), (SEND, N_W11B, 0, Z), (GOT, N_QKB, Z | X), (VEC, 2), (GOT, N_QKA, Z | Y),
+        (SEND, N_QKA, Z | Y, X), (GOT, N_VOB, Z), (SEND, N_VOB, Z, Y), (SEND, N_W10A, 0, Z),
+        (GOT, N_VOA, Z | X), (GOT, N_QKB, Z | Y), (SEND, N_QKB, Z | Y, X), (SEND, N_VOB, Z, X),
+        (SEND, N_W11B, 0, Y), (GOT, N_W11A, Z), (SEND, N_W10A, 0, Y), (VEC, 3), (SEND, N_W10B, 0, Z),
     ),
     unp0=(
-        (GOT, N_VOA, Z | X), (GOT, N_QKA, Z | Y), (SEND, N_VOB, Z, Y), (GOT, N_W11B, X), (SEND, N_W21B, 0, X),
-        (GOT, N_W11B, Z), (SEND, N_W11B, Z, X), (GOT, N_QKA, Z | X | Y), (SEND, N_W11A, 0, Z),
-        (SEND, N_VOA, 0, Y), (GOT, N_QKB, Z | Y | X), (GOT, N_QKA, Y), (SEND, N_VOB, 0, Y),
-        (GOT, N_QKA, X | Y), (SEND, N_W10A, 0, Y), (SEND, N_W10B, 0, Y), (GOT, N_VOB, Z | X),
-        (GOT, N_W10A, Z), (SEND, N_W10A, Z, X), (SEND, N_W11A, X, Z), (SEND, N_W11B, Z, Y), (WHOLE, N_QKA),
-        (WHOLE, N_QKB), (GOT, N_VOA, Z | Y), (SEND, N_VOA, Z | Y, X),
+        (DO, COT), (GOT, N_QKA, Z | Y | X), (GOT, N_VOA, Z | Y), (SEND, N_VOA, Z | Y, X), (GOT, N_W11B, Z),
+        (SEND, N_W10B, X, Z), (GOT, N_QKB, Z | Y | X), (GOT, N_VOB, Z | Y), (SEND, N_VOB, Z | Y, X),
+        (GOT, N_W11B, Y), (GOT, N_W10A, Z), (SEND, N_W11B, Y, Z), (GOT, N_W10A, Y), (WHOLE, N_QKA),
+        (WHOLE, N_QKB),
+    ),
+    projq=(
+        (GOT, N_VOB, Z | X), (SEND, N_W11A, Z, X),
     ),
     projk=(
-        (GOT, N_W11B, Z | X), (SEND, N_W11B, 0, Y),
+        (SEND, N_W11A, Z, Y),
     ),
     attend0=(
-        (GOT, N_W21B, X), (GOT, N_W10B, Z), (GOT, N_VOB, Z | Y), (SEND, N_VOB, Z | Y, X), (DO, COT),
+        (GOT, N_W10B, Z), (SEND, N_W10A, Y, Z),
     ),
     attend1=(
-        (GOT, N_VOA, Y), (SEND, N_VOA, Y, X), (GOT, N_VOB, Y), (SEND, N_VOB, Y, X),
+        (GOT, N_VOA, Z | Y | X), (SEND, N_W11B, Z, X),
     ),
     attend2=(
-        (GOT, N_W10A, Z | X), (SEND, N_W10B, Z, X), (GOT, N_W10A, Y), (SEND, N_W10A, Y, Z),
+        (SEND, N_W10B, Z, Y), (GOT, N_W10B, X | Z),
     ),
     attend3=(
-        (GOT, N_W11A, Z), (GOT, N_W10B, Y), (SEND, N_W10B, Y, Z),
+        (SEND, N_W21B, 0, Z),
     ),
     attend4=(
-        (GOT, N_VOA, Z | Y | X),
+        (GOT, N_VOB, Z | Y | X), (SEND, N_W10A, Z, X), (DO, COT_HERE), (SEND, N_W10B, X | Z, Y),
     ),
     attend5=(
-        (GOT, N_W11B, Z | Y), (SEND, N_W11B, Z | Y, X), (GOT, N_W11A, X | Z), (GOT, N_W11B, Y),
-        (SEND, N_W20A, 0, Z),
+        (GOT, N_W11B, Y | Z), (SEND, N_W20B, 0, Z),
     ),
     unp1=(
-        (GOT, N_VOB, Z | Y | X), (GOT, N_VOA, Y | X), (GOT, N_VOB, Y | X), (SEND, N_W11A, Z, Y),
-        (GOT, N_W10A, Y | Z), (SEND, N_W10A, Y | Z, X), (SEND, N_W20B, 0, Z), (WHOLE, N_VOA), (WHOLE, N_VOB),
-        (GOT, N_W10B, Z | X),
+        (WHOLE, N_VOA), (WHOLE, N_VOB), (GOT, N_W11A, Z | X), (SEND, N_W11B, Y | Z, X),
     ),
     projv=(
-        (SEND, N_W11A, X | Z, Y),
+        (GOT, N_W11A, Z | Y), (SEND, N_W11A, Z | X, Y), (DO, COTS_HERE),
     ),
     mix0=(
-        (SEND, N_W10A, Y, X), (SEND, N_W10B, Y, X),
-    ),
-    mix1=(
-        (GOT, N_W10B, Y | Z), (SEND, N_W10B, Y | Z, X), (SEND, N_W21A, 0, Z),
-    ),
-    mix3=(
-        (GOT, N_W11B, Z | Y | X), (SEND, N_W11B, Y, X), (SEND, N_W11A, 0, Y),
+        (GOT, N_W10A, Y | Z), (SEND, N_W21A, 0, Z),
+    ),
+    mix5=(
+        (GOT, N_W11B, Z | X),
     ),
     ao=(
-        (SEND, N_W21A, 0, X), (SEND, N_W11A, X, Y),
+        (SEND, N_W10A, Y | Z, X),
     ),
     ln2=(
-        (DO, COT_HERE),
+        (GOT, N_W10B, Z | Y), (SEND, N_W21A, 0, Y), (GOT, N_W21B, Z),
     ),
     expa0=(
-        (GOT, N_W10A, Y | Z | X), (GOT, N_W20A, Z), (SEND, N_W20A, Z, X), (SEND, N_W20A, Z, Y),
-        (SEND, N_W21B, 0, Z), (GOT, N_W11A, Z | Y), (GOT, N_W10B, Y | Z | X), (DO, COTS_HERE),
-        (GOT, N_W10A, Y | X), (GOT, N_W20B, Z), (SEND, N_W20B, Z, X), (SEND, N_W20B, Z, Y),
-        (SEND, N_W21B, X, Z), (GOT, N_W10B, Y | X), (GOT, N_W11A, X | Z | Y), (DO, N2S_HERE),
-        (SEND, N_W21B, 0, Y), (GOT, N_W11B, Y | X), (GOT, N_W11A, Y), (SEND, N_W21B, X, Y), (GOT, N_W21A, X),
-        (GOT, N_W11A, X | Y), (SEND, N_W20A, 0, Y),
+        (SEND, N_W20A, 0, Z), (SEND, N_W21B, Z, Y), (GOT, N_W10A, Z | X), (GOT, N_W10B, X | Z | Y),
+        (GOT, N_W20B, Z), (SEND, N_W20B, Z, X), (SEND, N_W20A, X, Z), (SEND, N_W20B, Z, Y), (DO, N2S_HERE),
+        (GOT, N_W11B, Y | Z | X), (SEND, N_W21B, Z, X), (GOT, N_W11A, Z | X | Y), (GOT, N_W21A, Z),
+        (GOT, N_W21A, Y), (SEND, N_W21A, Y, Z), (GOT, N_W10A, Y | Z | X), (SEND, N_W21A, Z, X),
     ),
     expa1=(
-        (GOT, N_W21A, Z), (SEND, N_W21A, Z, X), (SEND, N_W20B, 0, Y), (SEND, N_W21A, Z, Y),
-        (GOT, N_W20A, Z | X), (GOT, N_W20A, Z | Y), (SEND, N_W20A, Z | Y, X),
+        (GOT, N_W20A, Z), (SEND, N_W20A, Z, Y), (GOT, N_W21B, Z | Y),
     ),
     expb0=(
-        (GOT, N_W21B, Z),
+        (GOT, N_W20B, Z | X), (SEND, N_W20B, Z | X, Y), (SEND, N_W21B, Z | Y, X), (GOT, N_W20A, X | Z),
+        (GOT, N_W20B, Z | Y),
     ),
     expb1=(
-        (GOT, N_W20B, Z | X), (GOT, N_W20B, Z | Y), (SEND, N_W20B, Z | Y, X), (GOT, N_W21B, Y),
-        (SEND, N_W21B, Y, Z), (SEND, N_W20A, 0, X), (GOT, N_W21B, X | Y), (SEND, N_W21B, X | Y, Z),
-        (SEND, N_W20B, 0, X), (SEND, N_W21A, 0, Y),
+        (SEND, N_W20A, X | Z, Y), (GOT, N_W21B, Z | X),
     ),
     trY=(
-        (GOT, N_W21A, Z | X), (SEND, N_W21A, Z | X, Y), (GOT, N_W20A, Y), (SEND, N_W20A, Y, X),
-        (GOT, N_W21B, X | Z), (SEND, N_W21A, X, Y), (GOT, N_W20B, Y), (SEND, N_W20B, Y, X),
+        (GOT, N_W21A, Y | Z), (SEND, N_W21A, Y | Z, X), (GOT, N_W20A, Z | Y),
     ),
     gw2_0=(
-        (GOT, N_W20A, Z | Y | X),
+        (GOT, N_W21A, Z | X),
     ),
     gw2_1=(
-        (GOT, N_W21A, Z | Y), (GOT, N_W21B, Y | Z), (GOT, N_W20B, Z | Y | X),
+        (GOT, N_W20B, Z | X | Y),
     ),
     innb0=(
-        (GOT, N_W20A, X), (GOT, N_W21A, Z | X | Y), (GOT, N_W20B, X), (GOT, N_W21A, Y), (SUM, N_G20, 0),
-        (SUM, N_G21, 0), (GOT, N_W21B, X | Y | Z), (GOT, N_W20A, Y | X), (GOT, N_W21A, X | Y),
-        (GOT, N_W20B, Y | X),
+        (GOT, N_W21B, Z | Y | X), (SUM, N_G20, 0), (SUM, N_G21, 0), (GOT, N_W20A, X | Z | Y),
+        (GOT, N_W21A, Y | Z | X),
     ),
     gw1_0=(
         (DO, BACKS_HERE),
     ),
     hid=(
-        (SUM, N_G10, 0), (SUM, N_G11, 0),
-    ),
-    dO=(
+        (SUM, N_G10, 0), (SUM, N_G11A, 0), (SUM, N_G11B, 0), (SUM, N_G20, 1),
+    ),
+    ab0=(
+        (SUM, N_G11A, 1),
+    ),
+    ab2=(
         (SUM, N_G21, 1),
     ),
-    ab4=(
-        (SUM, N_G20, 1),
-    ),
-    ab5=(
-        (SUM, N_G10, 1), (SUM, N_G11, 1),
+    ab3=(
+        (SUM, N_AVO, 0), (SUM, N_G10, 1), (SUM, N_G11B, 1),
     ),
     gaqk=(
+        (SUM, N_G11A, 2),
+    ),
+    redb=(
         (SUM, N_G20, 2),
     ),
-    reda=(
-        (SUM, N_AVOB, 0), (SUM, N_G10, 2), (SUM, N_AVOA, 0),
-    ),
     outst=(
-        (SUM, N_G20, 3), (SUM, N_G11, 2), (SUM, N_AQKB, 0), (SUM, N_G21, 2), (SUM, N_AQKA, 0),
-        (DO, AHEADS_HERE),
+        (SUM, N_G11B, 2), (SUM, N_AQKB, 0), (SUM, N_AQKA, 0), (SUM, N_G10, 2), (DO, AHEADS_HERE),
+        (SUM, N_AVO, 1),
+    ),
+    inb=(
+        (SUM, N_G11A, 3), (DO, OUT), (SUM, N_G21, 2), (SUM, N_G20, 3),
     ),
     end=(
-        (SUM, N_AVOB, 1), (SUM, N_AVOA, 1), (SUM, N_G10, 3), (DO, OUT), (SUM, N_AQKB, 1), (SUM, N_AQKA, 1),
-        (SUM, N_G11, 3), (SMALL, 0), (SUM, N_AVOA, 2), (SMALL, 1), (DO, IG), (SUM, N_G21, 3),
-        (SUM, N_AVOB, 2), (SUM, N_AQKA, 2), (SMALL, 2), (DO, OUT_HERE), (SUM, N_AQKB, 2), (SUM, N_AVOA, 3),
-        (DO, IG_HERE), (SUM, N_AVOB, 3), (SUM, N_AQKB, 3), (SUM, N_AQKA, 3), (SMALL, 3),
+        (SUM, N_AQKA, 1), (SUM, N_AQKB, 1), (SUM, N_G10, 3), (DO, IG), (SUM, N_AVO, 2), (DO, OUT_HERE),
+        (SMALL, 0), (SUM, N_AQKB, 2), (SUM, N_AQKA, 2), (SMALL, 1), (SMALL, 2), (SUM, N_AVO, 3),
+        (DO, IG_HERE), (SUM, N_G21, 3), (SUM, N_AQKA, 3), (SUM, N_G11B, 3), (SMALL, 3), (SUM, N_AQKB, 3),
     ),
 )
 
@@ -278,149 +267,138 @@
         pl.semaphore_signal(barrier, inc=1, device_id=partner, device_id_type=MESH)
     pl.semaphore_wait(barrier, len(partners))
 
-    def offsets(axes):
-        return [(dy, dx, dz)
-                for dy in ((1,) if "y" in axes else (0,))
-                for dx in ((1,) if "x" in axes else (0,))
-                for dz in (range(1, zs) if "z" in axes else (0,))]
-
-    def owner(d):
-        dy, dx, dz = d
-        return (1 - y if dy else y, 1 - x if dx else x, z if isinstance(dz, int) and dz == 0 else z_at(zs - dz))
-
-    def moves(d, axis):
-        dy, dx, dz = d
-        if axis == "y":
-            return [(device(y_=1 - y), (1, dx, dz))]
-        if axis == "x":
-            return [(device(x_=1 - x), (dy, 1, dz))]
-        return [(device(z_=z_at(k)), (dy, dx, k)) for k in range(1, zs)]
-
-    def piece(n, d):
-        return n.u.at[owner(d) + (n.rows,)]
-
-    def ag_copy(n, ref, d, to):
-        slot = (d[0] * 2 + d[1]) * zs + d[2]
+    ME = {"y": y, "x": x, "z": z}
+
+    def before(n, axis, other):
+        return n.route.index(axis) < n.route.index(other)
+
+    def side(n, axes, all_z):
+        where = (1 - y if "y" in axes else y, 1 - x if "x" in axes else x, slice(None) if all_z else z)
+        return n.u.at[where + (n.rows,)]
+
+    def neighbour(axis):
+        return device(y_=1 - y) if axis == "y" else device(x_=1 - x)
+
+    def ag_copy(n, ref, axes, k, to):
+        slot = (("y" in axes) * 2 + ("x" in axes)) * zs + k
         return copy(ref, ref, ag_send.at[n.index, slot], ag_recv.at[n.index, slot], to)
 
     def core_copy(n, ref):
         return copy(ref, ref, core_send.at[n.index], core_recv.at[n.index], device(c_=1 - c))
 
+    def ag_sends(n, axes, axis):
+        axes = axes.replace("z", "")
+        if axis == "z":
+            ref = side(n, axes, False)
+            return [ag_copy(n, ref, axes, k, device(z_=z_at(k))) for k in range(1, zs)]
+        ref = side(n, axes, before(n, "z", axis))
+        return [ag_copy(n, ref, axes + axis, 0, neighbour(axis))]
+
     def ag_send_part(n, axes, axis):
-        for d in offsets(axes):
-            ref = piece(n, d)
-            for to, there in moves(d, axis):
-                ag_copy(n, ref, there, to).start()
+        for moved in ag_sends(n, axes, axis):
+            moved.start()
 
     def ag_wait_part(n, axes):
-        for d in offsets(axes):
-            ref = piece(n, d)
-            ag_copy(n, ref, d, device()).wait_recv()
-            if n.other is not None:
-                core_copy(n, ref).start()
+        last = max(axes, key=n.route.index)
+        axes = axes.replace("z", "")
+        if last == "z":
+            yy, xx = (1 - y if "y" in axes else y), (1 - x if "x" in axes else x)
+            for k in range(1, zs):
+                ag_copy(n, n.u.at[yy, xx, z_at(zs - k), n.rows], axes, k, device()).wait_recv()
+        else:
+            ag_copy(n, side(n, axes, before(n, "z", last)), axes, 0, device()).wait_recv()
+        if n.other is not None and (last == "z" or before(n, "z", last)):
+            core_copy(n, side(n, axes, True)).start()
 
     def ag_done(n):
         if n.other is not None:
             core_copy(n, n.other.at[:, :, :, n.rows]).wait_recv()
 
     def ag_drain(n):
-        own = piece(n, (0, 0, 0))
-        for d in [(dy, dx, dz) for dy in range(2) for dx in range(2) for dz in range(zs)][1:]:
-            ag_copy(n, own, d, device()).wait_send()
+        for axis in n.route:
+            earlier = [other for other in "yx" if before(n, other, axis)]
+            for some in range(2 ** len(earlier)):
+                axes = "".join(other for bit, other in enumerate(earlier) if some >> bit & 1)
+                for moved in ag_sends(n, axes, axis):
+                    moved.wait_send()
         if n.other is not None:
             core_copy(n, n.u.at[:, :, :, n.rows]).wait_send()
 
     AXES = "yxz"
 
-    def step_region(n, step, k):
-        where = []
-        for axis in AXES:
-            at_step = n.route.index(axis)
-            where.append(0 if at_step < step else (k if at_step == step else slice(None)))
-        return n.got.at[tuple(where) + (n.rows,)]
-
-    def step_groups(n, step):
+    def rs_groups(n, step):
         axis = n.route[step]
-        if axis == "y":
-            return [(1, 0, device(y_=1 - y))]
-        if axis == "x":
-            return [(1, 1, device(x_=1 - x))]
-        return [(k, 1 + k, device(z_=z_at(zs - k))) for k in range(1, zs)]
-
-    def rs_group(n, step, k, slot, to):
-        ref = step_region(n, step, k)
-        return copy(ref, ref, rs_send.at[n.index, slot], rs_recv.at[n.index, slot], to)
-
-    def step_offsets(n, step, k):
-        spans = []
-        for axis, size in zip(AXES, (2, 2, zs)):
-            at_step = n.route.index(axis)
-            spans.append((0,) if at_step < step else ((k,) if at_step == step else tuple(range(size))))
-        return spans
-
-    def add_terms(n, d, step):
-        dy, dx, dz = d
-        value = piece(n, d)[...].astype(F32)
+        if axis == "z":
+            return [(k, 1 + k, device(z_=z_at(zs - k))) for k in range(1, zs)]
+        return [(1, "yx".index(axis), neighbour(axis))]
+
+    def rs_where(n, step, k):
+        axis, out, land = n.route[step], [], []
+        for other in AXES:
+            if other == axis:
+                out.append(z_at(zs - k) if axis == "z" else 1 - ME[axis])
+                land.append(k)
+            elif before(n, other, axis):
+                out.append(ME[other])
+                land.append(0)
+            else:
+                out.append(slice(None))
+                land.append(slice(None))
+        return tuple(out) + (n.rows,), tuple(land) + (n.rows,)
+
+    def rs_copy(n, step, k, slot, to):
+        out, land = rs_where(n, step, k)
+        return copy(n.u.at[out], n.got.at[land], rs_send.at[n.index, slot], rs_recv.at[n.index, slot], to)
+
+    def rs_core(n):
+        return copy(n.other.at[:, :, :, n.rows], n.core_in.at[:, :, :, n.rows], rs_send.at[n.index, zs + 1],
+                    rs_recv.at[n.index, zs + 1], device(c_=1 - c))
+
+    def add_terms(n, place, step):
+        value = n.u[tuple(place) + (n.rows,)].astype(F32)
         if n.other is not None:
-            value = value + n.core_in[dy, dx, dz, n.rows].astype(F32)
+            value = value + n.core_in[tuple(place) + (n.rows,)].astype(F32)
         for axis in n.route[:step]:
-            if axis == "y":
-                value = value + n.got[1, dx, dz, n.rows].astype(F32)
-            elif axis == "x":
-                value = value + n.got[dy, 1, dz, n.rows].astype(F32)
-            else:
-                for k in range(1, zs):
-                    value = value + n.got[dy, dx, k, n.rows].astype(F32)
+            for k in range(1, zs) if axis == "z" else (1,):
+                where = [k if other == axis else (0 if before(n, other, axis) else at_place)
+                         for other, at_place in zip(AXES, place)]
+                value = value + n.got[tuple(where) + (n.rows,)].astype(F32)
         return value
 
     def rs_start(n):
-        for dy in range(2):
-            for dx in range(2):
-                for dz in range(zs):
-                    d = (dy, dx, dz)
-                    copy(n.other.at[owner(d) + (n.rows,)], n.core_in.at[d + (n.rows,)], rs_send.at[n.index, zs + 1],
-                         rs_recv.at[n.index, zs + 1], device(c_=1 - c)).start()
-
-    def rs_core_whole(n):
-        ref = n.core_in.at[:, :, :, n.rows]
-        return copy(ref, ref, rs_send.at[n.index, zs + 1], rs_recv.at[n.index, zs + 1], device(c_=1 - c))
+        rs_core(n).start()
 
     def rs_step(n, step):
         if step == 0 and n.other is not None:
-            rs_core_whole(n).wait_recv()
+            rs_core(n).wait_recv()
         if step > 0:
-            for k, slot, to in step_groups(n, step - 1):
-                rs_group(n, step - 1, k, slot, to).wait_recv()
+            for group in rs_groups(n, step - 1):
+                rs_copy(n, step - 1, *group).wait_recv()
         if step == 3:
-            n.total[n.rows, :] = add_terms(n, (0, 0, 0), 3)
+            n.total[n.rows, :] = add_terms(n, (y, x, z), 3)
             return
-        for k, slot, to in step_groups(n, step):
-            dys, dxs, dzs = step_offsets(n, step, k)
+        for k, slot, to in rs_groups(n, step):
+            out, _ = rs_where(n, step, k)
             if step > 0 or n.other is not None:
-
-                def body(e):
-                    for dy in dys:
-                        for dx in dxs:
-                            d = (dy, dx, dzs[0] if len(dzs) == 1 else e)
-                            piece(n, d)[...] = add_terms(n, d, step).astype(BF16)
-
-                if len(dzs) == 1:
-                    body(0)
+                spans = [range(2) if isinstance(at_place, slice) else (at_place,) for at_place in out[:2]]
+
+                def body(zz):
+                    for yy in spans[0]:
+                        for xx in spans[1]:
+                            n.u[yy, xx, zz, n.rows] = add_terms(n, (yy, xx, zz), step).astype(BF16)
+
+                if isinstance(out[2], slice):
+                    loop(zs, body)
                 else:
-                    loop(zs, body)
-            for dy in dys:
-                for dx in dxs:
-                    for dz in dzs:
-                        d = (dy, dx, dz)
-                        copy(piece(n, d), n.got.at[d + (n.rows,)], rs_send.at[n.index, slot],
-                             rs_recv.at[n.index, slot], to).start()
+                    body(out[2])
+            rs_copy(n, step, k, slot, to).start()
 
     def rs_drain(n):
         if n.other is not None:
-            rs_core_whole(n).wait_send()
+            rs_core(n).wait_send()
         for step in range(3):
-            for group in step_groups(n, step):
-                rs_group(n, step, *group).wait_send()
+            for group in rs_groups(n, step):
+                rs_copy(n, step, *group).wait_send()
 
     def small_sum(ref, slots, which):
         to = (device(y_=1 - y), device(c_=1 - c), device(x_=1 - x))
@@ -701,19 +679,13 @@
         AHEADS_HERE: lambda: ahead_swap.wait(),
     }
 
-    def core_own(first, last):
-        for n in units[first : last + 1]:
-            core_copy(n, piece(n, (0, 0, 0))).start()
-
     own_attention(0)
-    core_own(*QK)
     w1_swap.start()
     w2_swap.start()
     own_vectors()
     vec_steps[0]()
     run("own1")
     own_attention(1)
-    core_own(*VO)
     run("ownff")
     each_core(own_expand)
     each_core(own_reduce)
@@ -957,27 +929,30 @@
         transpose_rows(tc, s, n2[128 * s : 128 * s + 128, :])
     gp[768:1536, :] = dot_nn(tc[...], lane_tiles(o6)).astype(BF16)
 
+    def value_back(p):
+        grads_in, grad_value = d6[p], 0.0
+        for which in range(2):
+            grad_value = grad_value + dot_nn(pt[2 * p + which], half_of(grads_in, which))
+        tc[rows_of(p), :] = grad_value.T.astype(BF16)
+        o6[p] = grad_value.astype(BF16)
+
     def attend_back(p):
         rows = rows_of(p)
         queries, keys, values, grads_in = q6[p], k6[p], v6[p], d6[p]
         keys_t = turn(keys)
-        grad_query, grad_key, grad_value = [], 0.0, 0.0
+        grad_query, grad_key = [], 0.0
         for which in range(2):
-            probs = pt[2 * p + which]
-            wide = probs.astype(F32)
+            wide = pt[2 * p + which].astype(F32)
             grad_probs = dot_nt(half_of(values, which), grads_in)
             inner = jnp.sum(wide * grad_probs, axis=0, keepdims=True)
             grad_scores = (wide * (grad_probs - inner)).astype(BF16)
             grad_query.append(dot_nn(keys_t[64 * which : 64 * which + 64, :], grad_scores))
             grad_key = grad_key + dot_nn(grad_scores, half_of(queries, which))
-            grad_value = grad_value + dot_nn(probs, half_of(grads_in, which))
         grad_query = jnp.concatenate(grad_query, axis=0) * HEAD ** (-0.5)
         ta[rows, :] = grad_query.astype(BF16)
         tb[rows, :] = grad_key.T.astype(BF16)
-        tc[rows, :] = grad_value.T.astype(BF16)
         q6[p] = grad_query.T.astype(BF16)
         k6[p] = grad_key.astype(BF16)
-        v6[p] = grad_value.astype(BF16)
 
     def pack(p, first_row, second_row):
         def body(s):
@@ -998,7 +973,7 @@
 
         loop(zs, body)
 
-    parts("ab", 6, attend_back)
+    parts("av", 6, value_back)
     run("gav")
     for n in units[VO[0] : VO[1] + 1]:
         ag_drain(n)
@@ -1006,6 +981,7 @@
     pack(1, 0, 768)
     for n in grads[AVO[0] : AVO[1] + 1]:
         rs_start(n)
+    parts("ab", 6, attend_back)
     run("gaqk")
     for n in units[QK[0] : QK[1] + 1]:
         ag_drain(n)
@@ -1037,9 +1013,9 @@
     run("dn1")
     h1[...] = dot_nn(lane_tiles(q6), at[0])
     h1[...] += dot_nn(lane_tiles(k6), at[1])
-    h1[...] += dot_nn(lane_tiles(v6), at[2])
+    h1[...] += dot_nn(lane_tiles(o6), at[2])
     gvec[2:3, :] = jnp.sum(lane_tiles(q6).astype(F32), axis=0, keepdims=True)
-    gvec[3:4, :] = jnp.sum(lane_tiles(v6).astype(F32), axis=0, keepdims=True)
+    gvec[3:4, :] = jnp.sum(lane_tiles(o6).astype(F32), axis=0, keepdims=True)
 
     run("inb")
 

time: 162 us -> 158 us (0.975)
  Pallas kernels: 161 us -> 157 us
    pallas_call x1, Pallas kernels: 157 us -> 152 us  [layer(): pl.pallas_call(functools.partial(kernel, sub, zs), out_shape=(jax.ShapeDt...]
where the time goes in v1:
time: 158 us
  Pallas kernels  157 us (99%)
    pallas_call x1, Pallas kernels, layer(): pl.pallas_call(functools.partial(kernel, sub, zs), out_shape=(jax.ShapeDt...  152 us
    pallas_call x1, Pallas kernels, update(): pl.pallas_call(functools.partial(update_kernel, rates), out_shape=tuple(n...  4.67 us

profile of v1, /device:TPU:0, one launch (start us, length us, event | category | flops | bytes accessed | tf_op | source)
XLA Modules:
  0.0 158.0 jit_solution(4579492549578469435)
XLA Ops:
  0.6 152.5 %shard_map.254 = (bf16[4,128,768]{2,1,0:T(8,128)(2,1)}, bf16[4,128,768]{2,1,0:T(8,128)(2,1)}, f32[4,192,96]{2,1,0:T(8,128)}, f32[192,384]{1,0:T(8,128)}, f32[96,768]{1,0:T(8,128)}, /*index=5*/f32[3,96]{1,0:T(4,128)}) custom-call(bf16[4,128,768]{2,1,0:T(8,128)(2,1)} %refs_0_.2, bf16[4,128,768]{2,1,0:T(8,128)(2,1)} %refs_1_.2, s32[4,128]{1,0:T(4,128)} %refs_2_.2, ...), custom_call_target="tpu_custom_call" | custom-call | tf_op jit(solution)/shard_map/pallas_call | solution.py:1084
  153.1 4.7 %shard_map.255 = (f32[4,192,96]{2,1,0:T(8,128)}, f32[4,192,96]{2,1,0:T(8,128)}, f32[4,192,96]{2,1,0:T(8,128)}, f32[192,384]{1,0:T(8,128)}, f32[192,384]{1,0:T(8,...) custom-call(f32[4,192,96]{2,1,0:T(8,128)} %refs_0_.3, ...), custom_call_target="tpu_custom_call" | custom-call | tf_op jit(solution)/shard_map/pallas_call | solution.py:1151

commit v2 on v1

--- a/solution.py
+++ b/solution.py
@@ -221,9 +221,9 @@
 
 
 def kernel(sub, zs, *refs):
-    (tok, cot, mask_in, vec_in, a_in, w1_in, w2_in,
+    (tok, cot, mask_hbm, vec_hbm, a_hbm, w1_hbm, w2_hbm,
      out, ig, ga, g1, g2, gv,
-     ua, uw1, uw2, gw1, gw2, core_in, got,
+     mask_in, vec_in, a_in, w1_in, w2_in, ua, uw1, uw2, gw1, gw2, core_in, got,
      x_in, cot_in, stage, vec, gvec, vin, gin, narrow_rows,
      at, n1, q6, k6, v6, o6, pt, h1, acc, n2, act, gp, ta, tb, tc, d6,
      w1_other, w2_other, n2_other, cot_other, back_in, ahead_in,
@@ -265,7 +265,6 @@
     barrier = pltpu.get_barrier_semaphore()
     for partner in partners:
         pl.semaphore_signal(barrier, inc=1, device_id=partner, device_id_type=MESH)
-    pl.semaphore_wait(barrier, len(partners))
 
     ME = {"y": y, "x": x, "z": z}
 
@@ -528,10 +527,16 @@
         for j in range(3):
             vec[pl.ds(3 * i + j, 1), :] = rows[j : j + 1, :]
 
-    load_cot = pltpu.make_async_copy(cot, stage, local_sem.at[4])
+    loads = [pltpu.make_async_copy(src, dst, local_sem.at[4 + n]) for n, (src, dst) in enumerate((
+        (a_hbm, a_in), (vec_hbm, vec_in), (w1_hbm, w1_in), (w2_hbm, w2_in), (cot, stage), (mask_hbm, mask_in)
+    ))]
+    load_a, load_vec, load_w1, load_w2, load_cot, load_mask = loads
+    for load in loads:
+        load.start()
 
     def masked_cotangent():
         load_cot.wait()
+        load_mask.wait()
         eye = lax.broadcasted_iota(jnp.int32, (128, 128), 0) == lax.broadcasted_iota(jnp.int32, (128, 128), 1)
         for s in range(4):
             row = jnp.broadcast_to(mask_in[s : s + 1, :].astype(F32), (128, 128))
@@ -617,6 +622,8 @@
             actions[rest[0]]()
         else:
             (vec_steps if kind == VEC else gvec_steps)[rest[0] + 1]()
+            if (kind, rest[0]) == (SMALL, zs - 1):
+                finish_vectors()
 
     def run(part):
         for todo in PLAN.get(part, ()):
@@ -636,7 +643,6 @@
         for moved in copies:
             moved.wait_recv()
 
-    load_cot.start()
     own_tokens = pltpu.make_async_copy(tok.at[i], x_in.at[i], local_sem.at[0])
     own_tokens.start()
     own_cot = pltpu.make_async_copy(stage.at[i], cot_in.at[i], local_sem.at[1])
@@ -679,11 +685,16 @@
         AHEADS_HERE: lambda: ahead_swap.wait(),
     }
 
+    load_a.wait()
     own_attention(0)
+    load_vec.wait()
+    own_vectors()
+    load_w1.wait()
+    load_w2.wait()
+    pl.semaphore_wait(barrier, len(partners))
+    vec_steps[0]()
     w1_swap.start()
     w2_swap.start()
-    own_vectors()
-    vec_steps[0]()
     run("own1")
     own_attention(1)
     run("ownff")
@@ -1029,12 +1040,21 @@
     loop(4, input_back)
     gvec_steps[0]()
     own_grad.start()
-    run("end")
-    finish_vectors()
-    w1_back.wait()
-    each_core(join_expand)
-    w2_back.wait()
-    each_core(join_reduce)
+
+    def join():
+        w1_back.wait()
+        each_core(join_expand)
+        w2_back.wait()
+        each_core(join_reduce)
+
+    joined = False
+    for n, todo in enumerate(PLAN["end"]):
+        if not joined and n >= len(PLAN["end"]) - 3 and {2, 3, 4, 5} <= set(whole):
+            join()
+            joined = True
+        event(*todo)
+    if not joined:
+        join()
 
     own_out.wait()
     own_grad.wait()
@@ -1054,7 +1074,8 @@
     piece = (3 * columns, 128)
     vmem = lambda shape, dtype: pltpu.VMEM(shape, dtype)
     half = (2, 2, 2, zs) + piece
-    scratch = [vmem((2,) + half, BF16)] + [vmem(half, BF16)] * 4
+    scratch = [vmem(value.shape, value.dtype) for value in (span_mask, vectors, attention, expand, reduce_t)]
+    scratch += [vmem((2,) + half, BF16)] + [vmem(half, BF16)] * 4
     scratch += [vmem((2, 2, 2, zs) + piece, BF16), vmem((6, 2, 2, zs) + piece, BF16)]
     scratch += [vmem(tokens.shape, BF16)] * 3
     scratch += [vmem((16, width), F32)] * 2
@@ -1071,7 +1092,7 @@
     scratch += [tiles, flat, vmem((columns, width // 2), F32), vmem((2, width), F32), vmem((2, width), F32)]
     scratch += [vmem((6,) + piece, F32), vmem((width // 2, 2 * columns), F32)]
     scratch += [vmem((2 * columns, 2 * columns), F32), vmem(piece, F32)]
-    scratch += [pltpu.SemaphoreType.DMA((5,))]
+    scratch += [pltpu.SemaphoreType.DMA((10,))]
     gathered, summed = sum(map(len, GATHER_ROUTES)), sum(map(len, SUM_ROUTES))
     scratch += [pltpu.SemaphoreType.DMA((gathered, 4 * zs))] * 2
     scratch += [pltpu.SemaphoreType.DMA((gathered,))] * 2
@@ -1091,7 +1112,7 @@
             jax.ShapeDtypeStruct(reduce_t.shape, F32),
             jax.ShapeDtypeStruct(vectors.shape, F32),
         ),
-        in_specs=[anywhere] * 2 + [in_vmem] * 5,
+        in_specs=[anywhere] * 7,
         out_specs=(anywhere, anywhere) + (in_vmem,) * 4,
         scratch_shapes=scratch,
         compiler_params=pltpu.CompilerParams(

time: 158 us -> 157 us (level)
  no operation moved by 1% of the time
where the time goes in v2:
time: 157 us; the launch traced here: 156 us
  Pallas kernels  156 us (99%)
    pallas_call x1, Pallas kernels, layer(): pl.pallas_call(functools.partial(kernel, sub, zs), out_shape=(jax.ShapeDt...  151 us
    pallas_call x1, Pallas kernels, update(): pl.pallas_call(functools.partial(update_kernel, rates), out_shape=tuple(n...  4.67 us

profile of v2, /device:TPU:0, one launch (start us, length us, event | category | flops | bytes accessed | tf_op | source)
XLA Modules:
  0.0 156.5 jit_solution(9160027104770363520)
XLA Ops:
  0.6 151.0 %shard_map.254 = (bf16[4,128,768]{2,1,0:T(8,128)(2,1)}, bf16[4,128,768]{2,1,0:T(8,128)(2,1)}, f32[4,192,96]{2,1,0:T(8,128)}, f32[192,384]{1,0:T(8,128)}, f32[96,768]{1,0:T(8,128)}, /*index=5*/f32[3,96]{1,0:T(4,128)}) custom-call(bf16[4,128,768]{2,1,0:T(8,128)(2,1)} %refs_0_.2, bf16[4,128,768]{2,1,0:T(8,128)(2,1)} %refs_1_.2, s32[4,128]{1,0:T(4,128)} %refs_2_.2, ...), custom_call_target="tpu_custom_call" | custom-call | tf_op jit(solution)/shard_map/pallas_call | solution.py:1105
  151.6 4.7 %shard_map.255 = (f32[4,192,96]{2,1,0:T(8,128)}, f32[4,192,96]{2,1,0:T(8,128)}, f32[4,192,96]{2,1,0:T(8,128)}, f32[192,384]{1,0:T(8,128)}, f32[192,384]{1,0:T(8,...) custom-call(f32[4,192,96]{2,1,0:T(8,128)} %refs_0_.3, ...), custom_call_target="tpu_custom_call" | custom-call | tf_op jit(solution)/shard_map/pallas_call | solution.py:1172

commit v3 on v2

--- a/solution.py
+++ b/solution.py
@@ -51,7 +51,7 @@
 
 X, Y, Z = 1, 2, 4
 (N_QKA, N_QKB, N_VOA, N_VOB, N_W10A, N_W10B, N_W11A, N_W11B, N_W20A, N_W20B, N_W21A, N_W21B) = range(12)
-(N_AQKA, N_AQKB, N_AVO, N_G10, N_G11A, N_G11B, N_G20, N_G21) = range(8)
+(N_AQKA, N_AQKB, N_AVO, N_G10, N_G11A, N_G11B, N_G20, N_G21A, N_G21B) = range(9)
 QK, VO = (N_QKA, N_QKB), (N_VOA, N_VOB)
 AQK, AVO = (N_AQKA, N_AQKB), (N_AVO, N_AVO)
 SEND, GOT, WHOLE, SUM, VEC, SMALL, DO = range(7)
@@ -62,16 +62,16 @@
     ((Z, Y, X), (Z, Y, X),),
     ((Y, Z, X), (X, Z, Y),),
     ((Z, X, Y), (Y, Z, X),),
-    ((X, Z, Y), (Z, X, Y),),
-    ((Y, Z, X), (Z, Y, X),),
+    ((Z, X, Y), (Z, Y, X),),
+    ((Y, X, Z), (Z, X, Y),),
 )
 SUM_ROUTES = (
     ((Y, X, Z), (X, Z, Y),),
     ((Y, X, Z),),
     ((Y, X, Z),),
-    ((X, Z, Y), (X, Z, Y),),
+    ((Z, X, Y), (X, Z, Y),),
     ((Y, X, Z),),
-    ((Z, X, Y),),
+    ((Z, X, Y), (X, Z, Y),),
 )
 PLAN = dict(
     own1=(
@@ -81,126 +81,141 @@
         (DO, TOK), (SEND, N_VOA, 0, Z), (VEC, 0), (DO, SWAP_HERE),
     ),
     mask=(
-        (SEND, N_W10B, 0, X), (SEND, N_W20A, 0, X),
+        (SEND, N_W10B, 0, X), (SEND, N_W21A, 0, X),
     ),
     ln1=(
         (VEC, 1), (GOT, N_QKA, Z), (SEND, N_QKA, Z, X), (SEND, N_QKA, Z, Y), (SEND, N_VOB, 0, Z),
-        (GOT, N_W10B, X), (GOT, N_W20A, X), (GOT, N_QKB, Z), (SEND, N_QKB, Z, X), (SEND, N_QKB, Z, Y),
-        (SEND, N_W11A, 0, Z), (GOT, N_QKA, Z | X), (DO, TOK_HERE), (GOT, N_VOA, Z), (SEND, N_VOA, Z, X),
-        (SEND, N_VOA, Z, Y), (SEND, N_W11B, 0, Z), (GOT, N_QKB, Z | X), (VEC, 2), (GOT, N_QKA, Z | Y),
-        (SEND, N_QKA, Z | Y, X), (GOT, N_VOB, Z), (SEND, N_VOB, Z, Y), (SEND, N_W10A, 0, Z),
+        (GOT, N_W10B, X), (GOT, N_W21A, X), (VEC, 2), (GOT, N_QKB, Z), (SEND, N_QKB, Z, X),
+        (SEND, N_QKB, Z, Y), (SEND, N_W11A, 0, Z), (GOT, N_QKA, Z | X), (DO, TOK_HERE), (GOT, N_VOA, Z),
+        (SEND, N_VOA, Z, X), (SEND, N_VOA, Z, Y), (SEND, N_W10A, 0, Z), (GOT, N_QKB, Z | X),
+        (GOT, N_QKA, Z | Y), (SEND, N_QKA, Z | Y, X), (GOT, N_VOB, Z), (SEND, N_VOB, Z, Y), (VEC, 3),
+        (SEND, N_W10B, 0, Z),
+    ),
+    unp0=(
         (GOT, N_VOA, Z | X), (GOT, N_QKB, Z | Y), (SEND, N_QKB, Z | Y, X), (SEND, N_VOB, Z, X),
-        (SEND, N_W11B, 0, Y), (GOT, N_W11A, Z), (SEND, N_W10A, 0, Y), (VEC, 3), (SEND, N_W10B, 0, Z),
-    ),
-    unp0=(
-        (DO, COT), (GOT, N_QKA, Z | Y | X), (GOT, N_VOA, Z | Y), (SEND, N_VOA, Z | Y, X), (GOT, N_W11B, Z),
+        (SEND, N_W10A, 0, Y), (SEND, N_W11B, 0, Y), (GOT, N_W11A, Z), (SEND, N_W11B, 0, Z), (DO, COT),
+        (GOT, N_QKA, Z | Y | X), (GOT, N_VOA, Z | Y), (SEND, N_VOA, Z | Y, X), (GOT, N_W10A, Z),
         (SEND, N_W10B, X, Z), (GOT, N_QKB, Z | Y | X), (GOT, N_VOB, Z | Y), (SEND, N_VOB, Z | Y, X),
-        (GOT, N_W11B, Y), (GOT, N_W10A, Z), (SEND, N_W11B, Y, Z), (GOT, N_W10A, Y), (WHOLE, N_QKA),
+        (GOT, N_W10A, Y), (GOT, N_W10B, Z), (GOT, N_W11B, Y), (SEND, N_W10A, Y, Z), (WHOLE, N_QKA),
         (WHOLE, N_QKB),
     ),
     projq=(
-        (GOT, N_VOB, Z | X), (SEND, N_W11A, Z, X),
+        (GOT, N_VOB, Z | X),
     ),
     projk=(
-        (SEND, N_W11A, Z, Y),
+        (SEND, N_W11A, Z, X), (SEND, N_W11A, Z, Y),
     ),
     attend0=(
-        (GOT, N_W10B, Z), (SEND, N_W10A, Y, Z),
+        (GOT, N_W11B, Z),
     ),
     attend1=(
-        (GOT, N_VOA, Z | Y | X), (SEND, N_W11B, Z, X),
+        (SEND, N_W11B, Y, Z),
     ),
     attend2=(
+        (GOT, N_VOA, Z | Y | X), (SEND, N_W10A, Z, X),
+    ),
+    attend3=(
         (SEND, N_W10B, Z, Y), (GOT, N_W10B, X | Z),
     ),
-    attend3=(
+    attend4=(
         (SEND, N_W21B, 0, Z),
     ),
-    attend4=(
-        (GOT, N_VOB, Z | Y | X), (SEND, N_W10A, Z, X), (DO, COT_HERE), (SEND, N_W10B, X | Z, Y),
-    ),
     attend5=(
-        (GOT, N_W11B, Y | Z), (SEND, N_W20B, 0, Z),
+        (GOT, N_VOB, Z | Y | X), (SEND, N_W11B, Z, X),
     ),
     unp1=(
-        (WHOLE, N_VOA), (WHOLE, N_VOB), (GOT, N_W11A, Z | X), (SEND, N_W11B, Y | Z, X),
+        (DO, COT_HERE), (SEND, N_W10B, X | Z, Y), (GOT, N_W10A, Y | Z), (SEND, N_W20A, 0, Z), (WHOLE, N_VOA),
+        (WHOLE, N_VOB),
     ),
     projv=(
-        (GOT, N_W11A, Z | Y), (SEND, N_W11A, Z | X, Y), (DO, COTS_HERE),
+        (GOT, N_W11A, Z | X),
     ),
     mix0=(
-        (GOT, N_W10A, Y | Z), (SEND, N_W21A, 0, Z),
-    ),
-    mix5=(
-        (GOT, N_W11B, Z | X),
-    ),
-    ao=(
-        (SEND, N_W10A, Y | Z, X),
+        (SEND, N_W10A, Y | Z, X), (GOT, N_W11A, Z | Y), (SEND, N_W11A, Z | X, Y),
+    ),
+    mix1=(
+        (DO, COTS_HERE),
+    ),
+    mix3=(
+        (GOT, N_W11B, Y | Z),
+    ),
+    mix4=(
+        (SEND, N_W20B, 0, Z),
     ),
     ln2=(
-        (GOT, N_W10B, Z | Y), (SEND, N_W21A, 0, Y), (GOT, N_W21B, Z),
+        (GOT, N_W10A, Z | X),
     ),
     expa0=(
-        (SEND, N_W20A, 0, Z), (SEND, N_W21B, Z, Y), (GOT, N_W10A, Z | X), (GOT, N_W10B, X | Z | Y),
-        (GOT, N_W20B, Z), (SEND, N_W20B, Z, X), (SEND, N_W20A, X, Z), (SEND, N_W20B, Z, Y), (DO, N2S_HERE),
-        (GOT, N_W11B, Y | Z | X), (SEND, N_W21B, Z, X), (GOT, N_W11A, Z | X | Y), (GOT, N_W21A, Z),
-        (GOT, N_W21A, Y), (SEND, N_W21A, Y, Z), (GOT, N_W10A, Y | Z | X), (SEND, N_W21A, Z, X),
+        (SEND, N_W11B, Y | Z, X), (GOT, N_W10B, Z | Y), (SEND, N_W21A, 0, Y), (GOT, N_W21B, Z),
+        (SEND, N_W21B, Z, Y), (SEND, N_W21A, 0, Z), (GOT, N_W11B, Z | X), (SEND, N_W21B, Z, X),
+        (GOT, N_W10B, X | Z | Y), (DO, N2S_HERE), (GOT, N_W20A, Z), (SEND, N_W21A, X, Z),
+        (GOT, N_W10A, Y | Z | X), (SEND, N_W20A, Z, X), (GOT, N_W11A, Z | X | Y), (GOT, N_W21A, Y),
+        (GOT, N_W20B, Z), (SEND, N_W20B, Z, Y), (SEND, N_W20A, Z, Y), (SEND, N_W21A, Y, Z),
+        (GOT, N_W11B, Y | Z | X), (SEND, N_W21A, Y, X),
     ),
     expa1=(
-        (GOT, N_W20A, Z), (SEND, N_W20A, Z, Y), (GOT, N_W21B, Z | Y),
+        (SEND, N_W20B, Z, X), (GOT, N_W21B, Z | Y), (GOT, N_W21A, Z),
     ),
     expb0=(
-        (GOT, N_W20B, Z | X), (SEND, N_W20B, Z | X, Y), (SEND, N_W21B, Z | Y, X), (GOT, N_W20A, X | Z),
-        (GOT, N_W20B, Z | Y),
+        (GOT, N_W21B, Z | X), (SEND, N_W21B, Z | X, Y),
     ),
     expb1=(
-        (SEND, N_W20A, X | Z, Y), (GOT, N_W21B, Z | X),
+        (GOT, N_W20B, Z | Y), (SEND, N_W20B, Z | Y, X), (GOT, N_W21A, X | Z),
     ),
     trY=(
-        (GOT, N_W21A, Y | Z), (SEND, N_W21A, Y | Z, X), (GOT, N_W20A, Z | Y),
+        (GOT, N_W20A, Z | X), (SEND, N_W20A, Z | X, Y), (GOT, N_W21A, Y | X), (SEND, N_W21A, Y | X, Z),
     ),
     gw2_0=(
-        (GOT, N_W21A, Z | X),
-    ),
-    gw2_1=(
-        (GOT, N_W20B, Z | X | Y),
+        (GOT, N_W20A, Z | Y), (GOT, N_W21A, Y | Z),
     ),
     innb0=(
-        (GOT, N_W21B, Z | Y | X), (SUM, N_G20, 0), (SUM, N_G21, 0), (GOT, N_W20A, X | Z | Y),
-        (GOT, N_W21A, Y | Z | X),
+        (GOT, N_W20B, Z | X), (GOT, N_W21B, Z | X | Y), (SUM, N_G20, 0), (SUM, N_G21A, 0), (SUM, N_G21B, 0),
+        (GOT, N_W21A, Y | X | Z), (GOT, N_W20B, Z | Y | X), (GOT, N_W20A, Z | X | Y),
     ),
     gw1_0=(
+        (SUM, N_G21B, 1),
+    ),
+    gw1_1=(
         (DO, BACKS_HERE),
     ),
     hid=(
-        (SUM, N_G10, 0), (SUM, N_G11A, 0), (SUM, N_G11B, 0), (SUM, N_G20, 1),
+        (SUM, N_G10, 0), (SUM, N_G11A, 0), (SUM, N_G11B, 0),
+    ),
+    dO=(
+        (SUM, N_G21A, 1),
+    ),
+    gao=(
+        (SUM, N_G20, 1),
     ),
     ab0=(
+        (SUM, N_G21B, 2),
+    ),
+    ab1=(
+        (SUM, N_G11B, 1),
+    ),
+    ab3=(
+        (SUM, N_AVO, 0),
+    ),
+    ab5=(
+        (SUM, N_G20, 2), (SUM, N_G10, 1),
+    ),
+    gaqk=(
+        (SUM, N_G21A, 2),
+    ),
+    reda=(
         (SUM, N_G11A, 1),
     ),
-    ab2=(
-        (SUM, N_G21, 1),
-    ),
-    ab3=(
-        (SUM, N_AVO, 0), (SUM, N_G10, 1), (SUM, N_G11B, 1),
-    ),
-    gaqk=(
-        (SUM, N_G11A, 2),
-    ),
-    redb=(
-        (SUM, N_G20, 2),
-    ),
     outst=(
-        (SUM, N_G11B, 2), (SUM, N_AQKB, 0), (SUM, N_AQKA, 0), (SUM, N_G10, 2), (DO, AHEADS_HERE),
-        (SUM, N_AVO, 1),
+        (SUM, N_AQKB, 0), (SUM, N_AQKA, 0), (SUM, N_G10, 2), (DO, AHEADS_HERE),
     ),
     inb=(
-        (SUM, N_G11A, 3), (DO, OUT), (SUM, N_G21, 2), (SUM, N_G20, 3),
+        (SUM, N_G11A, 2), (SUM, N_G11B, 2),
     ),
     end=(
-        (SUM, N_AQKA, 1), (SUM, N_AQKB, 1), (SUM, N_G10, 3), (DO, IG), (SUM, N_AVO, 2), (DO, OUT_HERE),
-        (SMALL, 0), (SUM, N_AQKB, 2), (SUM, N_AQKA, 2), (SMALL, 1), (SMALL, 2), (SUM, N_AVO, 3),
-        (DO, IG_HERE), (SUM, N_G21, 3), (SUM, N_AQKA, 3), (SUM, N_G11B, 3), (SMALL, 3), (SUM, N_AQKB, 3),
+        (SUM, N_AVO, 1), (DO, OUT), (SUM, N_AQKB, 1), (SUM, N_G20, 3), (SUM, N_AQKA, 1), (SMALL, 0),
+        (SMALL, 1), (DO, IG), (SUM, N_AVO, 2), (SUM, N_G10, 3), (SUM, N_AQKA, 2), (SMALL, 2), (DO, OUT_HERE),
+        (SUM, N_AQKB, 2), (DO, IG_HERE), (SUM, N_AVO, 3), (SUM, N_G21B, 3), (SUM, N_G21A, 3),
+        (SUM, N_G11A, 3), (SUM, N_G11B, 3), (SUM, N_AQKA, 3), (SUM, N_AQKB, 3), (SMALL, 3),
     ),
 )
 

time: 157 us -> 158 us (level)
  no operation moved by 1% of the time
where the time goes in v3:
time: 158 us; the launch traced here: 157 us
  Pallas kernels  156 us (99%)
    pallas_call x1, Pallas kernels, layer(): pl.pallas_call(functools.partial(kernel, sub, zs), out_shape=(jax.ShapeDt...  151 us
    pallas_call x1, Pallas kernels, update(): pl.pallas_call(functools.partial(update_kernel, rates), out_shape=tuple(n...  4.67 us

profile of v3, /device:TPU:0, one launch (start us, length us, event | category | flops | bytes accessed | tf_op | source)
XLA Modules:
  0.0 156.9 jit_solution(3127921809523687707)
XLA Ops:
  0.6 151.4 %shard_map.254 = (bf16[4,128,768]{2,1,0:T(8,128)(2,1)}, bf16[4,128,768]{2,1,0:T(8,128)(2,1)}, f32[4,192,96]{2,1,0:T(8,128)}, f32[192,384]{1,0:T(8,128)}, f32[96,768]{1,0:T(8,128)}, /*index=5*/f32[3,96]{1,0:T(4,128)}) custom-call(bf16[4,128,768]{2,1,0:T(8,128)(2,1)} %refs_0_.2, bf16[4,128,768]{2,1,0:T(8,128)(2,1)} %refs_1_.2, s32[4,128]{1,0:T(4,128)} %refs_2_.2, ...), custom_call_target="tpu_custom_call" | custom-call | tf_op jit(solution)/shard_map/pallas_call | solution.py:1120
  152.0 4.7 %shard_map.255 = (f32[4,192,96]{2,1,0:T(8,128)}, f32[4,192,96]{2,1,0:T(8,128)}, f32[4,192,96]{2,1,0:T(8,128)}, f32[192,384]{1,0:T(8,128)}, f32[192,384]{1,0:T(8,...) custom-call(f32[4,192,96]{2,1,0:T(8,128)} %refs_0_.3, ...), custom_call_target="tpu_custom_call" | custom-call | tf_op jit(solution)/shard_map/pallas_call | solution.py:1187

commit v4 on v2

--- a/solution.py
+++ b/solution.py
@@ -51,7 +51,7 @@
 
 X, Y, Z = 1, 2, 4
 (N_QKA, N_QKB, N_VOA, N_VOB, N_W10A, N_W10B, N_W11A, N_W11B, N_W20A, N_W20B, N_W21A, N_W21B) = range(12)
-(N_AQKA, N_AQKB, N_AVO, N_G10, N_G11A, N_G11B, N_G20, N_G21) = range(8)
+(N_AQKA, N_AQKB, N_AVO, N_G10, N_G11A, N_G11B, N_G20, N_G21A, N_G21B) = range(9)
 QK, VO = (N_QKA, N_QKB), (N_VOA, N_VOB)
 AQK, AVO = (N_AQKA, N_AQKB), (N_AVO, N_AVO)
 SEND, GOT, WHOLE, SUM, VEC, SMALL, DO = range(7)
@@ -62,8 +62,8 @@
     ((Z, Y, X), (Z, Y, X),),
     ((Y, Z, X), (X, Z, Y),),
     ((Z, X, Y), (Y, Z, X),),
-    ((X, Z, Y), (Z, X, Y),),
-    ((Y, Z, X), (Z, Y, X),),
+    ((Z, X, Y), (Z, X, Y),),
+    ((Y, X, Z), (Z, Y, X),),
 )
 SUM_ROUTES = (
     ((Y, X, Z), (X, Z, Y),),
@@ -71,136 +71,146 @@
     ((Y, X, Z),),
     ((X, Z, Y), (X, Z, Y),),
     ((Y, X, Z),),
-    ((Z, X, Y),),
+    ((Z, X, Y), (X, Z, Y),),
 )
 PLAN = dict(
     own1=(
-        (SEND, N_QKA, 0, Z), (SEND, N_QKB, 0, Z),
+        (SEND, N_QKA, 0, Z),
     ),
     ownff=(
-        (DO, TOK), (SEND, N_VOA, 0, Z), (VEC, 0), (DO, SWAP_HERE),
+        (DO, TOK), (SEND, N_QKB, 0, Z), (VEC, 0), (DO, SWAP_HERE),
     ),
     mask=(
-        (SEND, N_W10B, 0, X), (SEND, N_W20A, 0, X),
+        (SEND, N_W10B, 0, X), (SEND, N_W21A, 0, X),
     ),
     ln1=(
-        (VEC, 1), (GOT, N_QKA, Z), (SEND, N_QKA, Z, X), (SEND, N_QKA, Z, Y), (SEND, N_VOB, 0, Z),
-        (GOT, N_W10B, X), (GOT, N_W20A, X), (GOT, N_QKB, Z), (SEND, N_QKB, Z, X), (SEND, N_QKB, Z, Y),
-        (SEND, N_W11A, 0, Z), (GOT, N_QKA, Z | X), (DO, TOK_HERE), (GOT, N_VOA, Z), (SEND, N_VOA, Z, X),
-        (SEND, N_VOA, Z, Y), (SEND, N_W11B, 0, Z), (GOT, N_QKB, Z | X), (VEC, 2), (GOT, N_QKA, Z | Y),
-        (SEND, N_QKA, Z | Y, X), (GOT, N_VOB, Z), (SEND, N_VOB, Z, Y), (SEND, N_W10A, 0, Z),
-        (GOT, N_VOA, Z | X), (GOT, N_QKB, Z | Y), (SEND, N_QKB, Z | Y, X), (SEND, N_VOB, Z, X),
-        (SEND, N_W11B, 0, Y), (GOT, N_W11A, Z), (SEND, N_W10A, 0, Y), (VEC, 3), (SEND, N_W10B, 0, Z),
+        (SEND, N_VOA, 0, Z), (VEC, 1), (GOT, N_QKA, Z), (SEND, N_QKA, Z, X), (GOT, N_W10B, X),
+        (SEND, N_QKA, Z, Y), (SEND, N_VOB, 0, Z), (GOT, N_W21A, X), (GOT, N_QKB, Z), (SEND, N_QKB, Z, X),
+        (SEND, N_QKB, Z, Y), (SEND, N_W11A, 0, Z), (GOT, N_QKA, Z | X), (DO, TOK_HERE), (GOT, N_VOA, Z),
+        (SEND, N_VOA, Z, X), (SEND, N_VOA, Z, Y), (GOT, N_QKB, Z | X), (VEC, 2), (GOT, N_QKA, Z | Y),
+        (SEND, N_QKA, Z | Y, X), (SEND, N_W11B, 0, Z), (GOT, N_VOB, Z), (SEND, N_VOB, Z, Y),
+        (GOT, N_VOA, Z | X), (GOT, N_QKB, Z | Y), (SEND, N_QKB, Z | Y, X), (SEND, N_W10A, 0, Z),
+        (GOT, N_W11A, Z), (VEC, 3),
     ),
     unp0=(
-        (DO, COT), (GOT, N_QKA, Z | Y | X), (GOT, N_VOA, Z | Y), (SEND, N_VOA, Z | Y, X), (GOT, N_W11B, Z),
-        (SEND, N_W10B, X, Z), (GOT, N_QKB, Z | Y | X), (GOT, N_VOB, Z | Y), (SEND, N_VOB, Z | Y, X),
-        (GOT, N_W11B, Y), (GOT, N_W10A, Z), (SEND, N_W11B, Y, Z), (GOT, N_W10A, Y), (WHOLE, N_QKA),
-        (WHOLE, N_QKB),
-    ),
-    projq=(
-        (GOT, N_VOB, Z | X), (SEND, N_W11A, Z, X),
+        (SEND, N_VOB, Z, X), (SEND, N_W11B, 0, Y), (SEND, N_W10A, 0, Y), (GOT, N_QKA, Z | Y | X),
+        (GOT, N_VOA, Z | Y), (SEND, N_W10B, 0, Z), (DO, COT), (GOT, N_W11B, Z), (SEND, N_VOA, Z | Y, X),
+        (GOT, N_QKB, Z | Y | X), (GOT, N_VOB, Z | Y), (SEND, N_W10B, X, Z), (GOT, N_W11B, Y),
+        (GOT, N_W10A, Z), (GOT, N_W10A, Y), (SEND, N_VOB, Z | Y, X), (WHOLE, N_QKA), (WHOLE, N_QKB),
     ),
     projk=(
-        (SEND, N_W11A, Z, Y),
+        (GOT, N_VOB, Z | X), (SEND, N_W11B, Y, Z),
     ),
     attend0=(
-        (GOT, N_W10B, Z), (SEND, N_W10A, Y, Z),
+        (GOT, N_W10B, Z),
     ),
     attend1=(
-        (GOT, N_VOA, Z | Y | X), (SEND, N_W11B, Z, X),
+        (SEND, N_W11A, Z, X), (SEND, N_W11A, Z, Y),
     ),
     attend2=(
-        (SEND, N_W10B, Z, Y), (GOT, N_W10B, X | Z),
+        (GOT, N_VOA, Z | Y | X), (SEND, N_W10A, Y, Z),
     ),
     attend3=(
-        (SEND, N_W21B, 0, Z),
+        (GOT, N_W10B, X | Z), (SEND, N_W11B, Z, X),
     ),
     attend4=(
-        (GOT, N_VOB, Z | Y | X), (SEND, N_W10A, Z, X), (DO, COT_HERE), (SEND, N_W10B, X | Z, Y),
+        (SEND, N_W10B, Z, Y), (GOT, N_VOB, Z | Y | X), (SEND, N_W20A, 0, Z),
     ),
     attend5=(
-        (GOT, N_W11B, Y | Z), (SEND, N_W20B, 0, Z),
+        (DO, COT_HERE), (GOT, N_W11B, Y | Z),
     ),
     unp1=(
-        (WHOLE, N_VOA), (WHOLE, N_VOB), (GOT, N_W11A, Z | X), (SEND, N_W11B, Y | Z, X),
+        (SEND, N_W10A, Z, X), (WHOLE, N_VOA), (WHOLE, N_VOB), (SEND, N_W10B, X | Z, Y),
     ),
     projv=(
-        (GOT, N_W11A, Z | Y), (SEND, N_W11A, Z | X, Y), (DO, COTS_HERE),
+        (GOT, N_W11A, Z | X), (SEND, N_W20B, 0, Z), (GOT, N_W11A, Z | Y),
     ),
     mix0=(
-        (GOT, N_W10A, Y | Z), (SEND, N_W21A, 0, Z),
-    ),
-    mix5=(
+        (DO, COTS_HERE), (GOT, N_W10A, Y | Z),
+    ),
+    mix2=(
+        (SEND, N_W11B, Y | Z, X),
+    ),
+    mix4=(
+        (SEND, N_W11A, Z | X, Y),
+    ),
+    ao=(
         (GOT, N_W11B, Z | X),
     ),
-    ao=(
-        (SEND, N_W10A, Y | Z, X),
-    ),
     ln2=(
-        (GOT, N_W10B, Z | Y), (SEND, N_W21A, 0, Y), (GOT, N_W21B, Z),
+        (SEND, N_W21B, 0, Z), (GOT, N_W10B, Z | Y),
     ),
     expa0=(
-        (SEND, N_W20A, 0, Z), (SEND, N_W21B, Z, Y), (GOT, N_W10A, Z | X), (GOT, N_W10B, X | Z | Y),
-        (GOT, N_W20B, Z), (SEND, N_W20B, Z, X), (SEND, N_W20A, X, Z), (SEND, N_W20B, Z, Y), (DO, N2S_HERE),
-        (GOT, N_W11B, Y | Z | X), (SEND, N_W21B, Z, X), (GOT, N_W11A, Z | X | Y), (GOT, N_W21A, Z),
-        (GOT, N_W21A, Y), (SEND, N_W21A, Y, Z), (GOT, N_W10A, Y | Z | X), (SEND, N_W21A, Z, X),
+        (GOT, N_W20A, Z), (SEND, N_W10A, Y | Z, X), (SEND, N_W21A, 0, Y), (GOT, N_W10A, Z | X),
+        (SEND, N_W21A, 0, Z), (SEND, N_W20A, Z, Y), (GOT, N_W10B, X | Z | Y), (GOT, N_W20B, Z),
+        (SEND, N_W20A, Z, X), (DO, N2S_HERE), (GOT, N_W11B, Y | Z | X), (SEND, N_W21A, X, Z),
+        (GOT, N_W11A, Z | X | Y), (GOT, N_W21B, Z), (SEND, N_W21B, Z, Y), (GOT, N_W21A, Y),
+        (SEND, N_W20B, Z, X), (GOT, N_W10A, Y | Z | X),
     ),
     expa1=(
-        (GOT, N_W20A, Z), (SEND, N_W20A, Z, Y), (GOT, N_W21B, Z | Y),
+        (SEND, N_W21A, Y, Z), (SEND, N_W20B, Z, Y), (GOT, N_W21A, Z), (GOT, N_W20A, Z | Y),
+        (SEND, N_W21A, Y, X),
     ),
     expb0=(
-        (GOT, N_W20B, Z | X), (SEND, N_W20B, Z | X, Y), (SEND, N_W21B, Z | Y, X), (GOT, N_W20A, X | Z),
+        (SEND, N_W21B, Z, X), (GOT, N_W20A, Z | X), (SEND, N_W20A, Z | X, Y),
+    ),
+    expb1=(
+        (GOT, N_W21A, X | Z), (GOT, N_W21B, Z | Y), (SEND, N_W21B, Z | Y, X), (GOT, N_W20B, Z | X),
+    ),
+    trY=(
+        (SEND, N_W20B, Z | X, Y), (GOT, N_W21A, Y | X), (SEND, N_W21A, Y | X, Z), (GOT, N_W21A, Y | Z),
         (GOT, N_W20B, Z | Y),
     ),
-    expb1=(
-        (SEND, N_W20A, X | Z, Y), (GOT, N_W21B, Z | X),
-    ),
-    trY=(
-        (GOT, N_W21A, Y | Z), (SEND, N_W21A, Y | Z, X), (GOT, N_W20A, Z | Y),
-    ),
-    gw2_0=(
-        (GOT, N_W21A, Z | X),
-    ),
     gw2_1=(
-        (GOT, N_W20B, Z | X | Y),
+        (GOT, N_W21B, Z | X), (GOT, N_W20A, Z | X | Y),
     ),
     innb0=(
-        (GOT, N_W21B, Z | Y | X), (SUM, N_G20, 0), (SUM, N_G21, 0), (GOT, N_W20A, X | Z | Y),
-        (GOT, N_W21A, Y | Z | X),
+        (GOT, N_W21A, Y | X | Z), (GOT, N_W21B, Z | Y | X), (SUM, N_G20, 0), (SUM, N_G21A, 0),
+        (SUM, N_G21B, 0), (GOT, N_W20B, Z | X | Y),
     ),
     gw1_0=(
         (DO, BACKS_HERE),
     ),
+    gw1_1=(
+        (SUM, N_G21B, 1),
+    ),
     hid=(
-        (SUM, N_G10, 0), (SUM, N_G11A, 0), (SUM, N_G11B, 0), (SUM, N_G20, 1),
+        (SUM, N_G10, 0), (SUM, N_G11A, 0), (SUM, N_G11B, 0),
+    ),
+    dO=(
+        (SUM, N_G20, 1), (SUM, N_G21A, 1),
     ),
     ab0=(
-        (SUM, N_G11A, 1),
-    ),
-    ab2=(
-        (SUM, N_G21, 1),
+        (SUM, N_G21B, 2), (SUM, N_G11A, 1),
     ),
     ab3=(
         (SUM, N_AVO, 0), (SUM, N_G10, 1), (SUM, N_G11B, 1),
     ),
-    gaqk=(
+    ab4=(
+        (SUM, N_G21B, 3),
+    ),
+    ab5=(
         (SUM, N_G11A, 2),
     ),
     redb=(
         (SUM, N_G20, 2),
     ),
+    reda=(
+        (SUM, N_G11B, 2),
+    ),
     outst=(
-        (SUM, N_G11B, 2), (SUM, N_AQKB, 0), (SUM, N_AQKA, 0), (SUM, N_G10, 2), (DO, AHEADS_HERE),
+        (SUM, N_AQKB, 0), (SUM, N_AQKA, 0), (SUM, N_G10, 2), (DO, AHEADS_HERE),
+    ),
+    dn1=(
         (SUM, N_AVO, 1),
     ),
     inb=(
-        (SUM, N_G11A, 3), (DO, OUT), (SUM, N_G21, 2), (SUM, N_G20, 3),
+        (SUM, N_G21A, 2), (SUM, N_G11A, 3), (SUM, N_G20, 3), (DO, OUT),
     ),
     end=(
-        (SUM, N_AQKA, 1), (SUM, N_AQKB, 1), (SUM, N_G10, 3), (DO, IG), (SUM, N_AVO, 2), (DO, OUT_HERE),
-        (SMALL, 0), (SUM, N_AQKB, 2), (SUM, N_AQKA, 2), (SMALL, 1), (SMALL, 2), (SUM, N_AVO, 3),
-        (DO, IG_HERE), (SUM, N_G21, 3), (SUM, N_AQKA, 3), (SUM, N_G11B, 3), (SMALL, 3), (SUM, N_AQKB, 3),
+        (SUM, N_AQKB, 1), (SUM, N_AQKA, 1), (SUM, N_G10, 3), (DO, IG), (SUM, N_AVO, 2), (SUM, N_AQKB, 2),
+        (DO, OUT_HERE), (SMALL, 0), (SUM, N_AQKA, 2), (SMALL, 1), (SMALL, 2), (SUM, N_AVO, 3), (DO, IG_HERE),
+        (SUM, N_AQKA, 3), (SUM, N_G11B, 3), (SMALL, 3), (SUM, N_G21A, 3), (SUM, N_AQKB, 3),
     ),
 )
 

time: 157 us -> 154 us (0.981)
  Pallas kernels: 156 us -> 153 us
    pallas_call x1, Pallas kernels: 151 us -> 149 us  [layer(): pl.pallas_call(functools.partial(kernel, sub, zs), out_shape=(jax.ShapeDt...]
where the time goes in v4:
time: 154 us
  Pallas kernels  153 us (99%)
    pallas_call x1, Pallas kernels, layer(): pl.pallas_call(functools.partial(kernel, sub, zs), out_shape=(jax.ShapeDt...  149 us
    pallas_call x1, Pallas kernels, update(): pl.pallas_call(functools.partial(update_kernel, rates), out_shape=tuple(n...  4.67 us

profile of v4, /device:TPU:0, one launch (start us, length us, event | category | flops | bytes accessed | tf_op | source)
XLA Modules:
  0.0 154.2 jit_solution(3153525766728934752)
XLA Ops:
  0.6 148.7 %shard_map.254 = (bf16[4,128,768]{2,1,0:T(8,128)(2,1)}, bf16[4,128,768]{2,1,0:T(8,128)(2,1)}, f32[4,192,96]{2,1,0:T(8,128)}, f32[192,384]{1,0:T(8,128)}, f32[96,768]{1,0:T(8,128)}, /*index=5*/f32[3,96]{1,0:T(4,128)}) custom-call(bf16[4,128,768]{2,1,0:T(8,128)(2,1)} %refs_0_.2, bf16[4,128,768]{2,1,0:T(8,128)(2,1)} %refs_1_.2, s32[4,128]{1,0:T(4,128)} %refs_2_.2, ...), custom_call_target="tpu_custom_call" | custom-call | tf_op jit(solution)/shard_map/pallas_call | solution.py:1115
  149.3 4.7 %shard_map.255 = (f32[4,192,96]{2,1,0:T(8,128)}, f32[4,192,96]{2,1,0:T(8,128)}, f32[4,192,96]{2,1,0:T(8,128)}, f32[192,384]{1,0:T(8,128)}, f32[192,384]{1,0:T(8,...) custom-call(f32[4,192,96]{2,1,0:T(8,128)} %refs_0_.3, ...), custom_call_target="tpu_custom_call" | custom-call | tf_op jit(solution)/shard_map/pallas_call | solution.py:1182
